TPU v7x, 32 devices: a whole 2x2x4 slice. The times are simulated.
32 devices in a mesh: dp: 8 (over z, y), seq: 4 (over x, core).
Axes of the slice: x: 2, y: 2, z: 4, core: 2. Of those that a mesh axis runs over, the one named last changes fastest.
Arguments:
- spatial_input_tokens: bfloat16 [16, 4, 64, 1152], P('dp', 'seq'), may hold values from -6 to 6
- upstream: bfloat16 [16, 4, 64, 1152], P('dp', None, 'seq'), may hold values from -6 to 6
- modulation: float32 [16, 6, 1152], P('dp'), may hold values from -3 to 3
- spatial_query_key_value: bfloat16 [3, 1152, 576], P(None, 'seq'), may hold values from -0.1875 to 0.1875
- spatial_output_weight: bfloat16 [576, 1152], P('seq'), may hold values from -0.25 to 0.25
- temporal_query_key_value: bfloat16 [3, 1152, 576], P(None, 'seq'), may hold values from -0.1875 to 0.1875
- temporal_output_weight: bfloat16 [576, 1152], P('seq'), may hold values from -0.25 to 0.25
- adapter_down_maps: float32 [2, 2, 32, 1152], replicated, may hold values from -0.1875 to 0.1875
- adapter_up_maps: float32 [2, 2, 32, 576], replicated, may hold values from -1 to 1
Outputs:
- grad_frames: bfloat16 [16, 4, 64, 1152], P('dp', 'seq')
- grad_down: float32 [2, 2, 32, 1152], replicated
- grad_up: float32 [2, 2, 32, 576], replicated
All inputs are finite; a program needn't handle non-finite values.
Results may differ from a plain program's by a relative error of at most 0.015.
Values may be sent and summed in bfloat16 or wider, within the bound.
A program may use at most 128 MiB of HBM per device.

v0:
```python
import jax
import jax.numpy as jnp
from jax import lax
from jax.sharding import PartitionSpec as P

LOCAL_HEADS = 8


EPSILON = 1e-06
full_precision = lax.Precision.HIGHEST


def head_norm(vectors):
    return (
        vectors * lax.rsqrt(jnp.mean(vectors * vectors, axis=-1, keepdims=True) + EPSILON)
    ).astype(jnp.bfloat16)


def attend(normed_query, normed_keys, values, temporal):
    factor = normed_query.shape[-1] ** (-0.5)
    if temporal:
        scores = jnp.einsum(
            "bfshd,bgshd->bshfg", normed_query, normed_keys, preferred_element_type=jnp.float32
        )
    else:
        scores = jnp.einsum(
            "bfshd,bfthd->bfhst", normed_query, normed_keys, preferred_element_type=jnp.float32
        )
    weights = jnp.exp(scores * factor)
    probabilities = (weights / jnp.sum(weights, axis=-1, keepdims=True)).astype(jnp.bfloat16)
    if temporal:
        attended = jnp.einsum(
            "bshfg,bgshd->bfshd", probabilities, values, preferred_element_type=jnp.float32
        )
    else:
        attended = jnp.einsum(
            "bfhst,bfthd->bfshd", probabilities, values, preferred_element_type=jnp.float32
        )
    return attended.astype(jnp.bfloat16)


def block(stream, modrows, proj_in, proj_out, down_maps, up_maps, temporal):
    features = stream.shape[-1]
    leading = stream.shape[:3]
    values32 = stream.astype(jnp.float32)
    center = values32 - jnp.mean(values32, axis=-1, keepdims=True)
    normed = center * lax.rsqrt(jnp.mean(center * center, axis=-1, keepdims=True) + EPSILON)
    shift_rows = modrows[:, 0][:, None, None, :]
    scale_rows = modrows[:, 1][:, None, None, :]
    gate_rows = modrows[:, 2][:, None, None, :]
    inputs = (normed * (1.0 + scale_rows) + shift_rows).astype(jnp.bfloat16)
    token_rows = inputs.reshape(-1, features)
    rows_wide = token_rows.astype(jnp.float32)
    low_query = jnp.dot(rows_wide, down_maps[0].T, precision=full_precision).astype(jnp.bfloat16)
    low_value = jnp.dot(rows_wide, down_maps[1].T, precision=full_precision).astype(jnp.bfloat16)
    query = jnp.dot(token_rows, proj_in[0], preferred_element_type=jnp.float32) + jnp.dot(
        low_query.astype(jnp.float32), up_maps[0], precision=full_precision
    )
    key_vectors = jnp.dot(token_rows, proj_in[1], preferred_element_type=jnp.float32)
    values = (
        jnp.dot(token_rows, proj_in[2], preferred_element_type=jnp.float32)
        + jnp.dot(low_value.astype(jnp.float32), up_maps[1], precision=full_precision)
    ).astype(jnp.bfloat16)
    inner_width = query.shape[-1]
    head_shape = (leading[0], leading[1], leading[2], LOCAL_HEADS, inner_width // LOCAL_HEADS)
    attended = attend(
        head_norm(query.reshape(head_shape)),
        head_norm(key_vectors.reshape(head_shape)),
        values.reshape(head_shape),
        temporal,
    )
    projected = jnp.dot(
        attended.reshape(-1, inner_width), proj_out, preferred_element_type=jnp.float32
    )
    return values32 + gate_rows * projected.reshape(leading[0], leading[1], leading[2], features)


def make_layer(modrows, proj_in, proj_out, temporal):

    def apply_layer(stream, down_maps, up_maps):
        result = block(stream, modrows, proj_in, proj_out, down_maps, up_maps, temporal)
        return result if temporal else result.astype(jnp.bfloat16)

    return apply_layer


def to_positions(hidden):
    return lax.all_to_all(hidden, "seq", split_axis=2, concat_axis=1, tiled=True)


def to_frames(cotangent):
    return lax.all_to_all(cotangent, "seq", split_axis=1, concat_axis=2, tiled=True)


def per_device(
    spatial_input_tokens,
    upstream,
    modulation,
    spatial_query_key_value,
    spatial_output_weight,
    temporal_query_key_value,
    temporal_output_weight,
    adapter_down_maps,
    adapter_up_maps,
):
    spatial_in, spatial_out, temporal_in, temporal_out = (
        lax.all_gather(spatial_query_key_value, "seq", axis=1, tiled=True),
        lax.all_gather(spatial_output_weight, "seq", axis=0, tiled=True),
        lax.all_gather(temporal_query_key_value, "seq", axis=1, tiled=True),
        lax.all_gather(temporal_output_weight, "seq", axis=0, tiled=True),
    )
    local_batch = spatial_input_tokens.shape[0]
    batch_spans = [(opening_row, opening_row + 1) for opening_row in range(local_batch)]
    factor = float(
        local_batch
        * lax.axis_size("dp")
        * spatial_input_tokens.shape[1]
        * lax.axis_size("seq")
        * spatial_input_tokens.shape[2]
    ) ** (-0.5)
    spatial_pullbacks = []
    hidden_parts = []
    for opening_row, closing_row in batch_spans:
        spatial_attention_layer = make_layer(
            modulation[opening_row:closing_row, 0:3], spatial_in, spatial_out, False
        )
        hidden, vector_jacobian = jax.vjp(
            spatial_attention_layer,
            spatial_input_tokens[opening_row:closing_row],
            adapter_down_maps[0],
            adapter_up_maps[0],
        )
        hidden_parts.append(hidden)
        spatial_pullbacks.append(vector_jacobian)
    temporal_down_map = jnp.zeros(adapter_down_maps.shape[1:], jnp.float32)
    temporal_up_map = jnp.zeros(adapter_up_maps.shape[1:], jnp.float32)
    back_parts = []
    for (opening_row, closing_row), hidden in zip(batch_spans, hidden_parts):
        position_major = to_positions(hidden)
        temporal_attention_layer = make_layer(
            modulation[opening_row:closing_row, 3:6], temporal_in, temporal_out, True
        )
        layer_output, vector_jacobian = jax.vjp(
            temporal_attention_layer, position_major, adapter_down_maps[1], adapter_up_maps[1]
        )
        back_hidden, part_down, part_up = vector_jacobian(
            upstream[opening_row:closing_row].astype(jnp.float32)
        )
        temporal_down_map = temporal_down_map + part_down
        temporal_up_map = temporal_up_map + part_up
        back_parts.append(back_hidden)
    spatial_down_map = jnp.zeros(adapter_down_maps.shape[1:], jnp.float32)
    spatial_up_map = jnp.zeros(adapter_up_maps.shape[1:], jnp.float32)
    grad_parts = []
    for back_hidden, vector_jacobian in zip(back_parts, spatial_pullbacks):
        by_frame = to_frames(back_hidden)
        grad_in, part_down, part_up = vector_jacobian(by_frame)
        spatial_down_map = spatial_down_map + part_down
        spatial_up_map = spatial_up_map + part_up
        grad_parts.append(grad_in)
    grad_frames = jnp.concatenate(grad_parts, axis=0)
    grad_down, grad_up = lax.psum(
        (
            jnp.stack([spatial_down_map, temporal_down_map]) * factor,
            jnp.stack([spatial_up_map, temporal_up_map]) * factor,
        ),
        ("dp", "seq"),
    )
    return (grad_frames, grad_down, grad_up)


def solution(mesh):
    placed = (
        P("dp", "seq", None, None),
        P("dp", None, "seq", None),
        P("dp", None, None),
        P(None, "seq", None),
        P("seq", None),
        P(None, "seq", None),
        P("seq", None),
        P(),
        P(),
    )
    return jax.shard_map(
        per_device,
        mesh=mesh,
        in_specs=placed,
        out_specs=(P("dp", "seq", None, None), P(), P()),
        check_vma=False,
    )
```

profile of v0, /device:TPU:1, one launch (start us, length us, event | category | flops | bytes accessed | tf_op | source)
XLA Modules:
  0.0 455.1 jit_solution(5757408440159298722)
XLA Ops:
  13.0 17.3 %all-gather.5.cloned.1.call-done = bf16[576,1152]{1,0:T(8,128)(2,1)} async-done(((bf16[144,1152]{1,0:T(8,128)(2,1)}), bf16[576,1152]{1,0:T(8,128)(2,1)}) %all-gather.5.cloned.1.call-update) | async-done | bytes 1327120 | tf_op jit(solution)/shard_map/all_gather | solution.py:110
  30.4 1.9 fusion.269
  34.4 33.3 %all-gather.7.cloned.1.call-done = bf16[3,1152,576]{2,1,0:T(8,128)(2,1)} async-done(((bf16[3,288,576]{2,1,0:T(8,128)(2,1)}), bf16[3,1152,576]{2,1,0:T(8,128)(2,1)}) %all-gather.7.cloned.1.call-update) | async-done | bytes 3981328 | tf_op jit(solution)/shard_map/all_gather | solution.py:107
  76.0 11.7 %all-gather.9.cloned.1.call-done = bf16[576,1152]{1,0:T(8,128)(2,1)} async-done(((bf16[144,1152]{1,0:T(8,128)(2,1)}), bf16[576,1152]{1,0:T(8,128)(2,1)}) %all-gather.9.cloned.1.call-update) | async-done | bytes 1327120 | tf_op jit(solution)/shard_map/all_gather | solution.py:108
  92.4 4.1 all-to-all-start
  96.6 5.7 %all-to-all-done = bf16[4,2,9216]{2,1,0:T(2,128)(2,1)S(1)} async-done(((bf16[4,2,9216]{2,1,0:T(2,128)(2,1)}), bf16[4,2,9216]{2,1,0:T(2,128)(2,1)S(1)}, u32[]{:S(2)}, u32[]{:S(2)}) %all-to-all-start) | async-done | bytes 147488 | tf_op jit(solution)/shard_map/all_to_all | solution.py:88
  104.4 22.0 %all-gather.11.cloned.1.call-done = bf16[3,1152,576]{2,1,0:T(8,128)(2,1)} async-done(((bf16[3,288,576]{2,1,0:T(8,128)(2,1)}), bf16[3,1152,576]{2,1,0:T(8,128)(2,1)}) %all-gather.11.cloned.1.call-update) | async-done | bytes 3981328 | tf_op jit(solution)/shard_map/all_gather | solution.py:109
  145.0 1.9 convolution_convert_fusion.9
  146.9 1.9 convolution_convert_fusion.10
  148.9 2.8 fusion.87
  155.2 3.7 all-to-all-start.1
  159.7 2.9 all-to-all-done.1
  165.5 1.9 fusion.50
  177.9 1.9 convolution_convert_fusion.6
  179.8 1.9 convolution_convert_fusion.7
  181.8 3.4 fusion.78
  188.8 2.5 fusion.58
  196.5 2.4 fusion.56
  211.9 4.6 %all-to-all-start.2 = ((bf16[4,2,9216]{2,1,0:T(2,128)(2,1)}), bf16[4,2,9216]{2,1,0:T(2,128)(2,1)S(1)}, u32[]{:S(2)}, u32[]{:S(2)}) async-start(bf16[4,2,9216]{2,1,0:T(2,128)(2,1)} %reshape.2082), calls=%async_computation.2 | async-start | bytes 294912 | tf_op jit(solution)/shard_map/all_to_all | solution.py:88
  217.3 2.9 all-to-all-done.2
  223.5 2.5 convolution_add_fusion.5
  230.5 2.5 fusion.60
  238.4 2.5 fusion.57
  276.5 2.0 convolution_convert_fusion.3
  278.5 1.9 convolution_convert_fusion.4
  280.5 2.8 fusion.86
  286.7 4.4 all-to-all-start.3
  307.0 1.9 convolution_convert_fusion
  309.0 1.9 convolution_convert_fusion.1
  311.0 2.1 fusion.84
  316.4 128.2 %all-reduce.19.cloned.1.call-done = (f32[2,2,32,1152]{3,2,1,0:T(8,128)}, f32[2,2,32,576]{3,2,1,0:T(8,128)}) async-done(((f32[2,2,32,1152]{3,2,1,0:T(8,128)}, f32[2,2,32,576]{3,2,1,0:T(8,128)}), (f32[2,2,32,1152]{3,2,1,0:T(8,128)}, f32[2,2,32,576]{3,2,1,0:T(8,128)})) %all-reduce.19.cloned.1.call-update) | async-done | bytes 884752 | tf_op jit(solution)/shard_map/psum | solution.py:162
  444.6 1.9 copy.558
  (498 shorter events, 153.0 us)
Async XLA Ops:
  7.2 23.2 %all-gather.5.cloned.1.call-start = ((), (), s32[]{:S(2)}) async-start(), calls=%async_computation.4 | async-start | bytes 1658880 | tf_op jit(solution)/shard_map/all_gather | solution.py:110
  7.9 59.8 %all-gather.7.cloned.1.call-start = ((), (), s32[]{:S(2)}) async-start(), calls=%async_computation.5 | async-start | bytes 5529600 | tf_op jit(solution)/shard_map/all_gather | solution.py:107
  8.7 79.1 %all-gather.9.cloned.1.call-start = ((), (), s32[]{:S(2)}) async-start(), calls=%async_computation.6 | async-start | bytes 1658880 | tf_op jit(solution)/shard_map/all_gather | solution.py:108
  9.4 117.0 %all-gather.11.cloned.1.call-start = ((), (), s32[]{:S(2)}) async-start(), calls=%async_computation.7 | async-start | bytes 5529600 | tf_op jit(solution)/shard_map/all_gather | solution.py:109
  11.0 21.3 %copy-start.89 = (f32[64]{0:T(128)}, f32[64]{0:T(128)S(1)}, u32[]{:S(2)}) copy-start(f32[64]{0:T(128)S(1)} %fusion.232) | copy-start | bytes 772
  11.7 120.9 %copy-start.85 = (f32[1152]{0:T(1024)}, f32[1152]{0:T(1024)S(1)}, u32[]{:S(2)}) copy-start(f32[1152]{0:T(1024)S(1)} %get-tuple-element.14) | copy-start | bytes 13828
  12.1 20.2 %copy-start.53 = (bf16[64,32]{0,1:T(8,128)(2,1)}, bf16[64,32]{0,1:T(8,128)(2,1)S(1)}, u32[]{:S(2)}) copy-start(bf16[64,32]{0,1:T(8,128)(2,1)S(1)} %convolution_convert_fusion.45) | copy-start | bytes 12292
  74.4 15.0 %copy-start.67 = (f32[64,8]{0,1:T(8,128)}, f32[64,8]{0,1:T(8,128)S(1)}, u32[]{:S(2)}) copy-start(f32[64,8]{0,1:T(8,128)S(1)} %copy.294) | copy-start | bytes 6148
  74.5 94.2 %copy-start.71 = (f32[64,8]{0,1:T(8,128)}, f32[64,8]{0,1:T(8,128)S(1)}, u32[]{:S(2)}) copy-start(f32[64,8]{0,1:T(8,128)S(1)} %get-tuple-element.71) | copy-start | bytes 6148
  92.4 9.9 %all-to-all-start = ((bf16[4,2,9216]{2,1,0:T(2,128)(2,1)}), bf16[4,2,9216]{2,1,0:T(2,128)(2,1)S(1)}, u32[]{:S(2)}, u32[]{:S(2)}) async-start(bf16[4,2,9216]{2,1,0:T(2,128)(2,1)} %reshape.2080), calls=%async_computation | async-start | bytes 294912 | tf_op jit(solution)/shard_map/all_to_all | solution.py:88
  102.5 30.1 %copy-start.95 = (f32[64]{0:T(128)}, f32[64]{0:T(128)S(1)}, u32[]{:S(2)}) copy-start(f32[64]{0:T(128)S(1)} %broadcast_multiply_fusion.2) | copy-start | bytes 772
  103.3 29.3 %copy-start.103 = (f32[64]{0:T(128)}, f32[64]{0:T(128)S(1)}, u32[]{:S(2)}) copy-start(f32[64]{0:T(128)S(1)} %get-tuple-element.38) | copy-start | bytes 772
  128.8 6.5 %copy-start.56 = (f32[4,16,8]{0,2,1:T(8,128)}, f32[4,16,8]{0,2,1:T(8,128)S(1)}, u32[]{:S(2)}) copy-start(f32[4,16,8]{0,2,1:T(8,128)S(1)} %copy.302) | copy-start | bytes 6148
  128.9 6.3 %copy-start.32 = (f32[4,16,8,72]{3,2,1,0:T(8,128)}, f32[4,16,8,72]{3,2,1,0:T(8,128)S(1)}, u32[]{:S(2)}) copy-start(f32[4,16,8,72]{3,2,1,0:T(8,128)S(1)} %reshape.2014) | copy-start | bytes 442372
  151.7 11.0 %copy-start = (bf16[576,1152]{1,0:T(8,128)(2,1)S(1)}, bf16[576,1152]{1,0:T(8,128)(2,1)}, u32[]{:S(2)}) copy-start(bf16[576,1152]{1,0:T(8,128)(2,1)} %all-gather.9.cloned.1.call-done) | copy-start | bytes 3981316
  155.2 7.4 %all-to-all-start.1 = ((bf16[1,4,16,1152]{3,2,0,1:T(8,128)(2,1)}), bf16[1,4,16,1152]{3,2,0,1:T(8,128)(2,1)S(1)}, u32[]{:S(2)}, u32[]{:S(2)}) async-start(bf16[1,4,16,1152]{3,2,0,1:T(8,128)(2,1)} %fusion.71), calls=%async_computation.1 | async-start | bytes 294912 | tf_op jit(solution)/shard_map/all_to_all | solution.py:92
  188.8 16.8 %copy-start.17 = (f32[64,8,72]{2,1,0:T(8,128)}, f32[64,8,72]{2,1,0:T(8,128)S(1)}, u32[]{:S(2)}) copy-start(f32[64,8,72]{2,1,0:T(8,128)S(1)} %reshape.2032) | copy-start | bytes 442372
  192.4 11.7 %copy-start.7 = (f32[1,1,64,8,72]{4,3,2,1,0:T(8,128)}, f32[1,1,64,8,72]{4,3,2,1,0:T(8,128)S(1)}, u32[]{:S(2)}) copy-start(f32[1,1,64,8,72]{4,3,2,1,0:T(8,128)S(1)} %reshape.2035) | copy-start | bytes 442372
  209.4 7.1 %copy-start.54 = (bf16[64,32]{0,1:T(8,128)(2,1)S(1)}, bf16[64,32]{0,1:T(8,128)(2,1)}, u32[]{:S(2)}) copy-start(bf16[64,32]{0,1:T(8,128)(2,1)} %copy-done.53) | copy-start | bytes 12292
  209.5 12.4 %copy-start.46 = (f32[1152]{0:T(1024)S(1)}, f32[1152]{0:T(1024)}, u32[]{:S(2)}) copy-start(f32[1152]{0:T(1024)} %get-tuple-element.20) | copy-start | bytes 13828
  209.5 12.4 %copy-start.83 = (f32[1152]{0:T(1024)S(1)}, f32[1152]{0:T(1024)}, u32[]{:S(2)}) copy-start(f32[1152]{0:T(1024)} %get-tuple-element.19) | copy-start | bytes 13828
  211.9 8.3 %all-to-all-start.2 = ((bf16[4,2,9216]{2,1,0:T(2,128)(2,1)}), bf16[4,2,9216]{2,1,0:T(2,128)(2,1)S(1)}, u32[]{:S(2)}, u32[]{:S(2)}) async-start(bf16[4,2,9216]{2,1,0:T(2,128)(2,1)} %reshape.2082), calls=%async_computation.2 | async-start | bytes 294912 | tf_op jit(solution)/shard_map/all_to_all | solution.py:88
  220.5 10.0 %copy-start.5 = (bf16[1,1,64,1152]{3,2,1,0:T(8,128)(2,1)}, bf16[1,1,64,1152]{3,2,1,0:T(8,128)(2,1)S(1)}, u32[]{:S(2)}) copy-start(bf16[1,1,64,1152]{3,2,1,0:T(8,128)(2,1)S(1)} %get-tuple-element.24) | copy-start | bytes 442372
  220.5 10.0 %copy-start.93 = (f32[64]{0:T(128)}, f32[64]{0:T(128)S(1)}, u32[]{:S(2)}) copy-start(f32[64]{0:T(128)S(1)} %broadcast_multiply_fusion) | copy-start | bytes 772
  221.9 8.6 %copy-start.101 = (f32[64]{0:T(128)}, f32[64]{0:T(128)S(1)}, u32[]{:S(2)}) copy-start(f32[64]{0:T(128)S(1)} %get-tuple-element.36) | copy-start | bytes 772
  223.5 7.0 %copy-start.47 = (f32[1152]{0:T(1024)S(1)}, f32[1152]{0:T(1024)}, u32[]{:S(2)}) copy-start(f32[1152]{0:T(1024)} %get-tuple-element.20) | copy-start | bytes 13828
  223.5 7.0 %copy-start.84 = (f32[1152]{0:T(1024)S(1)}, f32[1152]{0:T(1024)}, u32[]{:S(2)}) copy-start(f32[1152]{0:T(1024)} %get-tuple-element.19) | copy-start | bytes 13828
  246.3 6.4 %copy-start.39 = (f32[4,16,8]{2,1,0:T(8,128)S(1)}, f32[4,16,8]{2,1,0:T(8,128)}, u32[]{:S(2)}) copy-start(f32[4,16,8]{2,1,0:T(8,128)} %copy.358) | copy-start | bytes 6148
  254.6 8.9 %copy-start.6 = (bf16[1,1,64,1152]{3,2,1,0:T(8,128)(2,1)S(1)}, bf16[1,1,64,1152]{3,2,1,0:T(8,128)(2,1)}, u32[]{:S(2)}) copy-start(bf16[1,1,64,1152]{3,2,1,0:T(8,128)(2,1)} %copy-done.5) | copy-start | bytes 442372
  280.5 10.8 %copy-start.38 = (f32[1,32,1152]{2,1,0:T(8,128)S(1)}, f32[1,32,1152]{2,1,0:T(8,128)}, u32[]{:S(2)}) copy-start(f32[1,32,1152]{2,1,0:T(8,128)} %convolution_bitcast_fusion.3) | copy-start | bytes 442372
  286.7 8.1 %all-to-all-start.3 = ((bf16[1,4,16,1152]{3,2,0,1:T(8,128)(2,1)}), bf16[1,4,16,1152]{3,2,0,1:T(8,128)(2,1)S(1)}, u32[]{:S(2)}, u32[]{:S(2)}) async-start(bf16[1,4,16,1152]{3,2,0,1:T(8,128)(2,1)} %fusion.73), calls=%async_computation.3 | async-start | bytes 294912 | tf_op jit(solution)/shard_map/all_to_all | solution.py:92
  291.1 153.6 %all-reduce.19.cloned.1.call-start = ((), (), s32[]{:S(2)}) async-start(), calls=%async_computation.8 | async-start | bytes 1835008 | tf_op jit(solution)/shard_map/psum | solution.py:162
  (91 other events, 242.0 us)
Sparse Core Ops, SparseCore 0:
  9.6 20.7 all-gather.4
  31.9 35.7 all-gather.6
  69.3 18.3 all-gather.8
  89.2 37.1 all-gather.10
  315.4 129.1 all-reduce.18
where the time goes:
time: 464 us; the launch traced here: 455 us
  waiting for transfers between devices  228 us (49%)
  matrix products  108 us (23%)
  local copies, waits for them, and re-layouts  49.6 us (11%)
  other arithmetic  36 us (8%)
  starting transfers between devices  17.2 us (4%)
  between operations  16.3 us (4%)
    psum x1, waiting for transfers between devices, per_device(): lax.psum((jnp.stack([spatial_down_map, temporal_down_map]) * factor, jnp....  128 us
    all_gather x1, waiting for transfers between devices, per_device(): lax.all_gather(spatial_query_key_value, 'seq', axis=1, tiled=True)  33.3 us
    all_gather x1, waiting for transfers between devices, per_device(): lax.all_gather(temporal_query_key_value, 'seq', axis=1, tiled=True)  22 us
    dot_general x8, matrix products, block(): jnp.dot(token_rows, proj_in[2], preferred_element_type=jnp.float32)  19.6 us
    all_gather x1, waiting for transfers between devices, per_device(): lax.all_gather(temporal_output_weight, 'seq', axis=0, tiled=True)  17.3 us
    dot_general x8, matrix products, block(): jnp.dot(token_rows, proj_in[1], preferred_element_type=jnp.float32)  16.5 us
    dot_general x8, matrix products, block(): jnp.dot(token_rows, proj_in[0], preferred_element_type=jnp.float32)  15.6 us
    all_gather x1, waiting for transfers between devices, per_device(): lax.all_gather(spatial_output_weight, 'seq', axis=0, tiled=True)  11.7 us
  transfers between devices with their start and end apart: 9, of which 9 were waited for; matrix products, arithmetic and copies ran while one was open for 6% of the time, Pallas kernels for 0%

commit v1 on v0

v1 whole, which is shorter than its diff:
```python
import functools

import jax
import jax.numpy as jnp
from jax import lax
from jax.experimental import pallas as pl
from jax.experimental.pallas import tpu as pltpu
from jax.sharding import PartitionSpec as P

LOCAL_HEADS = 8
EPSILON = 1e-06
MESH = pl.DeviceIdType.MESH
BF, F32 = jnp.bfloat16, jnp.float32
VMEM = pl.BlockSpec(memory_space=pltpu.VMEM)
ANY = pl.BlockSpec(memory_space=pl.ANY)
VMEM_BYTES = 56 * 2**20


def nn(a, b):
    return lax.dot_general(a, b, (((1,), (0,)), ((), ())), preferred_element_type=F32)


def nt(a, b):
    return lax.dot_general(a, b, (((1,), (1,)), ((), ())), preferred_element_type=F32)


def tn(a, b):
    return lax.dot_general(a, b, (((0,), (0,)), ((), ())), preferred_element_type=F32)


def nt_full(a, b):
    return lax.dot_general(
        a, b, (((1,), (1,)), ((), ())), preferred_element_type=F32, precision=lax.Precision.HIGHEST
    )


def nn_full(a, b):
    return lax.dot_general(
        a, b, (((1,), (0,)), ((), ())), preferred_element_type=F32, precision=lax.Precision.HIGHEST
    )


class Layer:
    def __init__(self, z, mod_ref, row, down_ref, up_ref, layer, group_mask):
        self.tokens, self.width = z.shape
        self.batch = mod_ref.shape[0]
        self.mod_ref, self.row = mod_ref, row
        self.z = z.astype(F32)
        center = self.z - jnp.mean(self.z, axis=-1, keepdims=True)
        self.rstd = lax.rsqrt(jnp.mean(center * center, axis=-1, keepdims=True) + EPSILON)
        self.normed = center * self.rstd
        self.u = (self.normed * (1.0 + self.rows(1)) + self.rows(0)).astype(BF)
        rank = down_ref.shape[2]
        inner = up_ref.shape[3]
        self.rank, self.inner = rank, inner
        self.down = down_ref[layer].reshape(2 * rank, self.width).astype(BF)
        zero = jnp.zeros((rank, inner), BF)
        self.up_q = jnp.concatenate([up_ref[layer, 0].astype(BF), zero], axis=0)
        self.up_v = jnp.concatenate([zero, up_ref[layer, 1].astype(BF)], axis=0)
        self.head = inner // LOCAL_HEADS
        lane_head = lax.broadcasted_iota(jnp.int32, (1, inner), 1) // self.head
        self.head_rows = [(lane_head == h).astype(F32).astype(BF) for h in range(LOCAL_HEADS)]
        self.head_rows32 = [(lane_head == h).astype(F32) for h in range(LOCAL_HEADS)]
        spread_head = lax.broadcasted_iota(jnp.int32, (128, inner), 1) // self.head
        spread_row = lax.broadcasted_iota(jnp.int32, (128, inner), 0)
        self.spread = (spread_head == spread_row).astype(F32)
        self.group_mask = group_mask

    def rows(self, j):
        span = self.tokens // self.batch
        return jnp.concatenate(
            [
                jnp.broadcast_to(self.mod_ref[b, self.row + j][None, :], (span, self.width))
                for b in range(self.batch)
            ],
            axis=0,
        )

    def per_head(self, values):
        return nt_full(values, self.spread) * (1.0 / self.head)

    def to_lanes(self, values):
        return nn_full(values, self.spread)

    def big(self, values):
        return jnp.concatenate([values * m for m in self.head_rows], axis=0)

    def fold(self, values):
        t = self.tokens
        return sum(
            values[h * t : (h + 1) * t] * self.head_rows32[h] for h in range(LOCAL_HEADS)
        )

    def project(self, w_q, w_k, w_v):
        self.low = nt(self.u, self.down).astype(BF)
        self.q = nn(self.u, w_q[...]) + nn(self.low, self.up_q)
        self.k = nn(self.u, w_k[...])
        self.v = (nn(self.u, w_v[...]) + nn(self.low, self.up_v)).astype(BF)

    def attend(self):
        t = self.tokens
        self.r_q = self.to_lanes(lax.rsqrt(self.per_head(self.q * self.q) + EPSILON))
        self.r_k = self.to_lanes(lax.rsqrt(self.per_head(self.k * self.k) + EPSILON))
        self.qn = (self.q * self.r_q).astype(BF)
        self.kn_big = self.big((self.k * self.r_k).astype(BF))
        self.v_big = self.big(self.v)
        scores = nt(self.qn, self.kn_big)
        factor = self.head ** (-0.5)
        probs = []
        for h in range(LOCAL_HEADS):
            e = jnp.where(self.group_mask, jnp.exp(scores[:, h * t : (h + 1) * t] * factor), 0.0)
            probs.append(e / jnp.sum(e, axis=-1, keepdims=True))
        self.probs32 = probs
        self.probs = jnp.concatenate([p.astype(BF) for p in probs], axis=1)

    def output(self, w_o):
        att = nn(self.probs, self.v_big).astype(BF)
        return self.z + self.rows(2) * nn(att, w_o[...])

    def backward(self, dout, w_q, w_k, w_v, w_o):
        t = self.tokens
        datt = nt((self.rows(2) * dout).astype(BF), w_o[...]).astype(BF)
        dprobs = nt(datt, self.v_big)
        dv = self.fold(tn(self.probs, datt)).astype(BF)
        factor = self.head ** (-0.5)
        ds = []
        for h in range(LOCAL_HEADS):
            dp = dprobs[:, h * t : (h + 1) * t].astype(BF).astype(F32)
            p = self.probs32[h]
            ds.append((p * (dp - jnp.sum(p * dp, axis=-1, keepdims=True)) * factor).astype(BF))
        ds = jnp.concatenate(ds, axis=1)
        dqn = nn(ds, self.kn_big).astype(BF).astype(F32)
        dkn = self.fold(tn(ds, self.qn)).astype(BF).astype(F32)

        def norm_back(d, x, r):
            xn = x * r
            return r * (d - xn * self.to_lanes(self.per_head(d * xn)))

        dq = norm_back(dqn, self.q, self.r_q).astype(BF)
        dk = norm_back(dkn, self.k, self.r_k).astype(BF)
        dlow = (nt(dq, self.up_q) + nt(dv, self.up_v)).astype(BF)
        du = nt(dq, w_q[...]) + nt(dk, w_k[...]) + nt(dv, w_v[...]) + nn(dlow, self.down)
        du = du.astype(BF).astype(F32)
        grad_down = tn(dlow, self.u)
        grad_up = jnp.concatenate(
            [tn(self.low, dq)[: self.rank], tn(self.low, dv)[self.rank :]], axis=0
        )
        dn = du * (1.0 + self.rows(1))
        dz = dout + self.rstd * (
            dn
            - jnp.mean(dn, axis=-1, keepdims=True)
            - self.normed * jnp.mean(dn * self.normed, axis=-1, keepdims=True)
        )
        return dz, grad_down, grad_up


def spatial_mask(tokens, positions):
    row = lax.broadcasted_iota(jnp.int32, (tokens, tokens), 0)
    col = lax.broadcasted_iota(jnp.int32, (tokens, tokens), 1)
    return row // positions == col // positions


def temporal_mask(tokens, batch, positions):
    row = lax.broadcasted_iota(jnp.int32, (tokens, tokens), 0)
    col = lax.broadcasted_iota(jnp.int32, (tokens, tokens), 1)
    span = tokens // batch
    return (row // span == col // span) & (row % positions == col % positions)


def spatial_forward_kernel(positions, z, mod, down, up, w_in, w_out, hidden, q, k, v, low):
    layer = Layer(z[...], mod, 0, down, up, 0, spatial_mask(z.shape[0], positions))
    layer.project(w_in.at[0], w_in.at[1], w_in.at[2])
    layer.attend()
    hidden[...] = layer.output(w_out).astype(BF)
    q[...], k[...], v[...], low[...] = layer.q, layer.k, layer.v, layer.low


def temporal_kernel(positions, z, upstream, mod, down, up, w_in, w_out, dz, g_down, g_up):
    layer = Layer(
        z[...], mod, 3, down, up, 1, temporal_mask(z.shape[0], mod.shape[0], positions)
    )
    layer.project(w_in.at[0], w_in.at[1], w_in.at[2])
    layer.attend()
    grad, g_down[...], g_up[...] = layer.backward(
        upstream[...].astype(F32), w_in.at[0], w_in.at[1], w_in.at[2], w_out
    )
    dz[...] = grad.astype(BF)


def spatial_backward_kernel(
    positions, z, cotangent, q, k, v, low, mod, down, up, w_in, w_out, dz, g_down, g_up
):
    layer = Layer(z[...], mod, 0, down, up, 0, spatial_mask(z.shape[0], positions))
    layer.q, layer.k, layer.v, layer.low = q[...], k[...], v[...], low[...]
    layer.attend()
    grad, g_down[...], g_up[...] = layer.backward(
        cotangent[...].astype(F32), w_in.at[0], w_in.at[1], w_in.at[2], w_out
    )
    dz[...] = grad.astype(BF)


def vmem_call(kernel, out_shape, *operands):
    return pl.pallas_call(
        kernel,
        out_shape=out_shape,
        in_specs=[VMEM] * len(operands),
        out_specs=[VMEM] * len(out_shape),
        compiler_params=pltpu.CompilerParams(vmem_limit_bytes=VMEM_BYTES),
    )(*operands)


def gather_kernel(
    n_dp, n_seq, in_s, out_s, in_t, out_t, all_in_s, all_out_s, all_in_t, all_out_t, own_sem,
    sib_send, sib_recv, x_send, x_recv, y_send, y_recv, fwd_send, fwd_recv,
):
    d, s = lax.axis_index("dp"), lax.axis_index("seq")
    chips = n_seq // 2
    chip, core = s // 2, s % 2
    other_core = 2 * chip + 1 - core
    pair = d + 1 - 2 * (d % 2)

    def at(chip_index):
        return 2 * lax.rem(chip_index + chips, chips)

    barrier = pltpu.get_barrier_semaphore()
    greet = [(d, other_core), (pair, s)] + [(d, at(chip + j) + core) for j in range(1, chips)]
    for target in greet:
        pl.semaphore_signal(barrier, inc=1, device_id=target, device_id_type=MESH)
    pl.semaphore_wait(barrier, len(greet))

    def source(piece):
        mine, out = (in_s, out_s) if piece < 4 else (in_t, out_t)
        return mine.at[piece % 4] if piece % 4 < 3 else out

    def place(piece, shard):
        full, out = (all_in_s, all_out_s) if piece < 4 else (all_in_t, all_out_t)
        return full.at[piece % 4, shard] if piece % 4 < 3 else out.at[shard]

    def remote(src, dst, send, recv, target):
        return pltpu.make_async_remote_copy(
            src_ref=src, dst_ref=dst, send_sem=send, recv_sem=recv,
            device_id=target, device_id_type=MESH,
        )

    def own(piece):
        return pltpu.make_async_copy(source(piece), place(piece, s), own_sem.at[piece])

    def to_sibling(piece):
        return remote(
            source(piece), place(piece, s), sib_send.at[piece], sib_recv.at[piece], (d, other_core)
        )

    def across(j, piece):
        return remote(
            source(piece), place(piece, s), x_send.at[j - 1, piece], x_recv.at[j - 1, piece],
            (d, at(chip + j) + core),
        )

    def relay(j, piece, sems, target):
        held = place(piece, at(chip - j) + core)
        return remote(held, held, sems[0].at[j - 1, piece], sems[1].at[j - 1, piece], target)

    def to_pair(j, piece):
        return relay(j, piece, (y_send, y_recv), (pair, s))

    def to_core(j, piece):
        return relay(j, piece, (fwd_send, fwd_recv), (d, other_core))

    def run(half):
        layers = [0, 4]
        first = [[base + 2 * half, base + 2 * half + 1] for base in layers]
        second = [[base + 2 - 2 * half, base + 3 - 2 * half] for base in layers]
        for layer in range(2):
            for piece in first[layer]:
                for j in range(1, chips):
                    across(j, piece).start()
        for piece in range(8):
            to_sibling(piece).start()
            own(piece).start()
        for layer in range(2):
            for piece in first[layer]:
                for j in range(1, chips):
                    across(j, piece).wait_recv()
                    to_pair(j, piece).start()
                    to_core(j, piece).start()
            for piece in second[layer]:
                for j in range(1, chips):
                    to_pair(j, piece).wait_recv()
                    to_core(j, piece).start()
        for piece in range(8):
            to_sibling(piece).wait()
            own(piece).wait()
            for j in range(1, chips):
                to_core(j, piece).wait()
        for layer in range(2):
            for piece in first[layer]:
                for j in range(1, chips):
                    across(j, piece).wait_send()
                    to_pair(j, piece).wait_send()

    for half in range(2):
        pl.when(d % 2 == half)(functools.partial(run, half))


def gather_weights(n_dp, n_seq, weights):
    in_s, out_s, in_t, out_t = weights
    links = max(n_seq // 2 - 1, 1)
    dma = pltpu.SemaphoreType.DMA
    shapes = []
    for w in weights:
        full = w.shape[:-2] + (n_seq,) + w.shape[-2:]
        shapes.append(jax.ShapeDtypeStruct(full, BF))
    gathered = pl.pallas_call(
        functools.partial(gather_kernel, n_dp, n_seq),
        out_shape=shapes,
        in_specs=[ANY] * 4,
        out_specs=[ANY] * 4,
        scratch_shapes=[dma((8,))] * 3 + [dma((links, 8))] * 6,
        compiler_params=pltpu.CompilerParams(collective_id=0, has_side_effects=True),
    )(*weights)
    return [
        g.reshape(g.shape[:-3] + (g.shape[-3] * g.shape[-2], g.shape[-1])) for g in gathered
    ]


def sum_kernel(
    n_dp, n_seq, x, out, wide, got_seq, part, got_dp, full, s1, r1, s2, r2, s3, r3, s4, r4
):
    d, s = lax.axis_index("dp"), lax.axis_index("seq")

    def seq_at(j):
        return lax.rem(s + j, n_seq)

    def dp_at(j):
        return lax.rem(d + j, n_dp)

    barrier = pltpu.get_barrier_semaphore()
    for j in range(1, n_seq):
        pl.semaphore_signal(barrier, inc=1, device_id=(d, seq_at(j)), device_id_type=MESH)
    for j in range(1, n_dp):
        pl.semaphore_signal(barrier, inc=1, device_id=(dp_at(j), s), device_id_type=MESH)
    wide[...] = x[...].astype(BF)
    pl.semaphore_wait(barrier, n_seq - 1 + n_dp - 1)

    def exchange(count, source, dest, send, recv, target):
        copies = [
            pltpu.make_async_remote_copy(
                src_ref=source(j), dst_ref=dest(j), send_sem=send.at[j - 1],
                recv_sem=recv.at[j - 1], device_id=target(j), device_id_type=MESH,
            )
            for j in range(1, count)
        ]
        for copy in copies:
            copy.start()
        return copies

    to_seq = lambda j: (d, seq_at(j))
    to_dp = lambda j: (dp_at(j), s)
    pending = exchange(
        n_seq, lambda j: wide.at[seq_at(j)], lambda j: got_seq.at[j - 1], s1, r1, to_seq
    )
    for copy in pending:
        copy.wait_recv()
    total = x[s]
    for j in range(1, n_seq):
        total = total + got_seq[j - 1].astype(F32)
    part[...] = total.astype(BF)
    more = exchange(n_dp, lambda j: part.at[dp_at(j)], lambda j: got_dp.at[j - 1], s2, r2, to_dp)
    for copy in more:
        copy.wait_recv()
    mine = part[d].astype(F32)
    for j in range(1, n_dp):
        mine = mine + got_dp[j - 1].astype(F32)
    full[s, d] = mine.astype(BF)
    pending += more
    more = exchange(n_dp, lambda j: full.at[s, d], lambda j: full.at[s, d], s3, r3, to_dp)
    for copy in more:
        copy.wait_recv()
    pending += more
    more = exchange(n_seq, lambda j: full.at[s], lambda j: full.at[s], s4, r4, to_seq)
    for copy in more:
        copy.wait_recv()
    out[...] = full[...].astype(F32)
    for copy in pending + more:
        copy.wait_send()


def sum_everywhere(n_dp, n_seq, flat):
    total = flat.shape[0]
    unit = 16 * 128
    devices = n_dp * n_seq
    rows = -(-total // (devices * unit)) * 16
    padded = jnp.pad(flat, (0, devices * rows * 128 - total))
    shape = (n_seq, n_dp, rows, 128)
    dma = pltpu.SemaphoreType.DMA
    seq_sem, dp_sem = dma((n_seq - 1,)), dma((n_dp - 1,))
    summed = pl.pallas_call(
        functools.partial(sum_kernel, n_dp, n_seq),
        out_shape=jax.ShapeDtypeStruct(shape, F32),
        in_specs=[VMEM],
        out_specs=VMEM,
        scratch_shapes=[
            pltpu.VMEM(shape, BF),
            pltpu.VMEM((n_seq - 1,) + shape[1:], BF),
            pltpu.VMEM(shape[1:], BF),
            pltpu.VMEM((n_dp - 1,) + shape[2:], BF),
            pltpu.VMEM(shape, BF),
            seq_sem, seq_sem, dp_sem, dp_sem, dp_sem, dp_sem, seq_sem, seq_sem,
        ],
        compiler_params=pltpu.CompilerParams(
            collective_id=1, has_side_effects=True, vmem_limit_bytes=VMEM_BYTES
        ),
    )(padded.reshape(shape))
    return summed.reshape(-1)[:total]


def per_device(n_dp, n_seq, z, upstream, mod, in_s, out_s, in_t, out_t, down, up):
    w_in_s, w_out_s, w_in_t, w_out_t = gather_weights(n_dp, n_seq, (in_s, out_s, in_t, out_t))
    batch, frames_here, positions, width = z.shape
    frames = frames_here * n_seq
    positions_here = positions // n_seq
    inner, rank = up.shape[3], up.shape[2]
    tokens = batch * frames_here * positions
    factor = float(batch * n_dp * frames * positions) ** (-0.5)
    shape = jax.ShapeDtypeStruct
    z_rows = z.reshape(tokens, width)
    hidden, q, k, v, low = vmem_call(
        functools.partial(spatial_forward_kernel, positions),
        [
            shape((tokens, width), BF), shape((tokens, inner), F32), shape((tokens, inner), F32),
            shape((tokens, inner), BF), shape((tokens, 2 * rank), BF),
        ],
        z_rows, mod, down, up, w_in_s, w_out_s,
    )
    by_position = lax.all_to_all(
        hidden.reshape(z.shape), "seq", split_axis=2, concat_axis=1, tiled=True
    )
    grads = [
        shape((tokens, width), BF), shape((2 * rank, width), F32), shape((2 * rank, inner), F32)
    ]
    back, down_t, up_t = vmem_call(
        functools.partial(temporal_kernel, positions_here), grads,
        by_position.reshape(tokens, width), upstream.reshape(tokens, width), mod, down, up,
        w_in_t, w_out_t,
    )
    by_frame = lax.all_to_all(
        back.reshape(batch, frames, positions_here, width), "seq", split_axis=1, concat_axis=2,
        tiled=True,
    )
    grad, down_s, up_s = vmem_call(
        functools.partial(spatial_backward_kernel, positions), grads,
        z_rows, by_frame.reshape(tokens, width), q, k, v, low, mod, down, up, w_in_s, w_out_s,
    )
    flat = jnp.concatenate([a.reshape(-1) for a in (down_s, down_t, up_s, up_t)]) * factor
    flat = sum_everywhere(n_dp, n_seq, flat)
    cut = down.size
    return grad.reshape(z.shape), flat[:cut].reshape(down.shape), flat[cut:].reshape(up.shape)


def solution(mesh):
    placed = (
        P("dp", "seq", None, None),
        P("dp", None, "seq", None),
        P("dp", None, None),
        P(None, "seq", None),
        P("seq", None),
        P(None, "seq", None),
        P("seq", None),
        P(),
        P(),
    )
    return jax.shard_map(
        functools.partial(per_device, mesh.shape["dp"], mesh.shape["seq"]),
        mesh=mesh,
        in_specs=placed,
        out_specs=(P("dp", "seq", None, None), P(), P()),
        check_vma=False,
    )
```

time: 464 us -> 185 us (0.40); the launches traced: 455 us -> 184 us
  waiting for transfers between devices: 228 us -> 4.46 us
  Pallas kernels: 0 us -> 152 us
  matrix products: 108 us -> 0 us
  other arithmetic: 36 us -> 0.06 us
  local copies, waits for them, and re-layouts: 49.6 us -> 13.9 us
  between operations: 16.3 us -> 0.7 us
  starting transfers between devices: 17.2 us -> 3.99 us
  blocking collectives: 0 us -> 9.34 us
    pallas_call x0 -> x5, Pallas kernels: none -> 152 us  [the longest x1 90.9 us: gather_weights(): pl.pallas_call(functools.partial(gather_kernel, n_dp, n_seq), out_shape=s...]
    psum x1 -> x0, waiting for transfers between devices: 128 us -> none  [per_device(): lax.psum((jnp.stack([spatial_down_map, temporal_down_map]) * factor, jnp....]
    dot_general x100 -> x0, matrix products: 108 us -> none  [the longest x8 19.6 us: block(): jnp.dot(token_rows, proj_in[2], preferred_element_type=jnp.float32)]
    all_gather x4 -> x0, waiting for transfers between devices: 84.4 us -> none  [the longest x1 33.3 us: per_device(): lax.all_gather(spatial_query_key_value, 'seq', axis=1, tiled=True)]
    reshape x34 -> x8, local copies, waits for them, and re-layouts: 21.2 us -> 7.82 us  [the longest x4 3.04 us: per_device(): a.reshape(-1)]
    all_to_all x4 -> x1, starting transfers between devices: 16.8 us -> 3.99 us  [per_device(): lax.all_to_all(back.reshape(batch, frames, positions_here, width), 'seq',...]
    all_to_all x0 -> x1, blocking collectives: none -> 9.34 us  [per_device(): lax.all_to_all(hidden.reshape(z.shape), 'seq', split_axis=2, concat_axis=...]
    reduce_sum x21 -> x0, other arithmetic: 8.86 us -> none  [the longest x6 3.2 us: block(): center = values32 - jnp.mean(values32, axis=-1, keepdims=True)]
  transfers between devices with their start and end apart: 9 -> 1, of which waited for: 9 -> 1; matrix products, arithmetic and copies ran while one was open for 6% -> 1% of each run, Pallas kernels for 0% -> 0%
where the time goes in v1:
time: 185 us; the launch traced here: 184 us
  Pallas kernels  152 us (82%)
  local copies, waits for them, and re-layouts  13.9 us (8%)
  blocking collectives  9.34 us (5%)
  waiting for transfers between devices  4.46 us (2%)
  starting transfers between devices  3.99 us (2%)
    pallas_call x1, Pallas kernels, gather_weights(): pl.pallas_call(functools.partial(gather_kernel, n_dp, n_seq), out_shape=s...  90.9 us
    pallas_call x3, Pallas kernels, vmem_call(): pl.pallas_call(kernel, out_shape=out_shape, in_specs=[VMEM] * len(operand...  31.4 us
    pallas_call x1, Pallas kernels, sum_everywhere(): pl.pallas_call(functools.partial(sum_kernel, n_dp, n_seq), out_shape=jax....  29.7 us
    all_to_all x1, blocking collectives, per_device(): lax.all_to_all(hidden.reshape(z.shape), 'seq', split_axis=2, concat_axis=...  9.34 us
    all_to_all x1, waiting for transfers between devices, per_device(): lax.all_to_all(back.reshape(batch, frames, positions_here, width), 'seq',...  4.46 us
    all_to_all x1, starting transfers between devices, per_device(): lax.all_to_all(back.reshape(batch, frames, positions_here, width), 'seq',...  3.99 us
  transfers between devices with their start and end apart: 1, of which 1 were waited for; matrix products, arithmetic and copies ran while one was open for 1% of the time, Pallas kernels for 0%

profile of v1, /device:TPU:1, one launch (start us, length us, event | category | flops | bytes accessed | tf_op | source)
XLA Modules:
  0.0 184.5 jit_solution(13333728622018776469)
XLA Ops:
  0.6 1.5 copy.16.mod
  2.1 90.9 %shard_map.112 = (bf16[3,4,288,576]{3,2,1,0:T(8,128)(2,1)}, bf16[4,144,1152]{2,1,0:T(8,128)(2,1)}, bf16[3,4,288,576]{3,2,1,0:T(8,128)(2,1)}, bf16[4,144,1152]{2,1,0:T(8,128)(2,1)}) custom-call(bf16[3,288,576]{2,1,0:T(8,128)(2,1)} %in_s.1, bf16[144,1152]{1,0:T(8,128)(2,1)} %out_s.1, bf16[3,288,576]{2,1,0:T(8,128)(2,1)} %in_t.1, bf16[144,1152]{1,0:T(8,128)(2,1)} %out_t.1), custom_call_target="tpu_custom_call" | custom-call | tf_op jit(solution)/shard_map/pallas_call | solution.py:313
  93.0 7.9 %shard_map.113 = (bf16[128,1152]{1,0:T(8,128)(2,1)}, f32[128,576]{1,0:T(8,128)}, f32[128,576]{1,0:T(8,128)}, bf16[128,576]{1,0:T(8,128)(2,1)}, bf16[128,64]{1,0:T(8,128)(2,1)}) custom-call(bf16[128,1152]{1,0:T(8,128)(2,1)} %bitcast.26, f32[2,6,1152]{2,1,0:T(8,128)} %copy.16.mod, f32[2,2,32,1152]{3,2,1,0:T(8,128)} %down.5, f32[2,2,32,576]{3,2,1,0:T(8,128)} %up.5, ...), custom_call_target="tpu_custom_call" | custom-call | tf_op jit(solution)/shard_map/pallas_call | solution.py:203
  100.9 1.3 copy.17
  102.2 9.3 %all_to_all.8 = bf16[2,1,64,1152]{3,0,1,2:T(2,128)(2,1)S(1)} all-to-all(bf16[2,1,64,1152]{3,0,1,2:T(2,128)(2,1)S(1)} %copy.17), channel_id=1, replica_groups=mesh['dp'=8,'seq'=4] {'seq'}, dimensions={2} | all-to-all | bytes 589824 | tf_op jit(solution)/shard_map/all_to_all | solution.py:435
  111.5 0.7 copy.18
  112.3 12.3 %shard_map.114 = (bf16[128,1152]{1,0:T(8,128)(2,1)}, f32[64,1152]{1,0:T(8,128)}, f32[64,576]{1,0:T(8,128)}) custom-call(bf16[128,1152]{1,0:T(8,128)(2,1)} %bitcast.25, bf16[128,1152]{1,0:T(8,128)(2,1)} %bitcast.28, f32[2,6,1152]{2,1,0:T(8,128)} %copy.16.mod, f32[2,2,32,1152]{3,2,1,0:T(8,128)} %down.5, f32[2,2,32,576]{3,2,1,0:T(8,128)} %up.5, ...), custom_call_target="tpu_custom_call" | custom-call | tf_op jit(solution)/shard_map/pallas_call | solution.py:203
  124.6 0.0 copy-start
  124.6 1.7 copy.20
  126.3 4.0 %all-to-all-start.1 = ((bf16[2,4,16,1152]{3,2,0,1:T(8,128)(2,1)}), bf16[2,4,16,1152]{3,2,0,1:T(8,128)(2,1)S(1)}, u32[]{:S(2)}, u32[]{:S(2)}) async-start(bf16[2,4,16,1152]{3,2,0,1:T(8,128)(2,1)} %copy.20), calls=%async_computation.1 | async-start | bytes 589824 | tf_op jit(solution)/shard_map/all_to_all | solution.py:446
  130.3 1.0 reshape.85
  131.3 0.0 copy-done
  131.4 4.5 %all-to-all-done.1 = bf16[2,4,16,1152]{3,2,0,1:T(8,128)(2,1)S(1)} async-done(((bf16[2,4,16,1152]{3,2,0,1:T(8,128)(2,1)}), bf16[2,4,16,1152]{3,2,0,1:T(8,128)(2,1)S(1)}, u32[]{:S(2)}, u32[]{:S(2)}) %all-to-all-start.1) | async-done | bytes 294944 | tf_op jit(solution)/shard_map/all_to_all | solution.py:446
  135.8 0.8 copy.21
  136.6 11.2 %shard_map.115 = (bf16[128,1152]{1,0:T(8,128)(2,1)}, f32[64,1152]{1,0:T(8,128)}, f32[64,576]{1,0:T(8,128)}) custom-call(bf16[128,1152]{1,0:T(8,128)(2,1)} %bitcast.27, bf16[128,1152]{1,0:T(8,128)(2,1)} %bitcast.24, f32[128,576]{1,0:T(8,128)} %get-tuple-element.24.q, f32[128,576]{1,0:T(8,128)} %get-tuple-element.25.k, bf16[128,576]{1,0:T(8,128)(2,1)} %get-tuple-element.26.v, ...), custom_call_target="tpu_custom_call" | custom-call | tf_op jit(solution)/shard_map/pallas_call | solution.py:203
  147.8 1.0 reshape.84
  148.8 1.0 reshape.82
  149.8 0.1 maximum_multiply_fusion
  149.9 1.0 pad.4
  150.9 29.7 %shard_map.116 = f32[4,8,64,128]{3,2,1,0:T(8,128)} custom-call(f32[4,8,64,128]{3,2,1,0:T(8,128)} %bitcast.20), custom_call_target="tpu_custom_call" | custom-call | tf_op jit(solution)/shard_map/pallas_call | solution.py:397
  180.6 1.0 slice.12
  181.6 1.1 slice.11
  182.7 0.9 reshape.88
  183.6 0.8 reshape.89
  (1 shorter events, 0.0 us)
Async XLA Ops:
  124.6 6.8 %copy-start = (f32[64,1152]{1,0:T(8,128)S(1)}, f32[64,1152]{1,0:T(8,128)}, u32[]{:S(2)}) copy-start(f32[64,1152]{1,0:T(8,128)} %get-tuple-element.30) | copy-start | bytes 884740
  126.3 9.5 %all-to-all-start.1 = ((bf16[2,4,16,1152]{3,2,0,1:T(8,128)(2,1)}), bf16[2,4,16,1152]{3,2,0,1:T(8,128)(2,1)S(1)}, u32[]{:S(2)}, u32[]{:S(2)}) async-start(bf16[2,4,16,1152]{3,2,0,1:T(8,128)(2,1)} %copy.20), calls=%async_computation.1 | async-start | bytes 589824 | tf_op jit(solution)/shard_map/all_to_all | solution.py:446

commit v2 on v1

--- a/solution.py
+++ b/solution.py
@@ -93,9 +93,9 @@
 
     def project(self, w_q, w_k, w_v):
         self.low = nt(self.u, self.down).astype(BF)
-        self.q = nn(self.u, w_q[...]) + nn(self.low, self.up_q)
-        self.k = nn(self.u, w_k[...])
-        self.v = (nn(self.u, w_v[...]) + nn(self.low, self.up_v)).astype(BF)
+        self.q = nn(self.u, w_q()) + nn(self.low, self.up_q)
+        self.k = nn(self.u, w_k())
+        self.v = (nn(self.u, w_v()) + nn(self.low, self.up_v)).astype(BF)
 
     def attend(self):
         t = self.tokens
@@ -115,11 +115,16 @@
 
     def output(self, w_o):
         att = nn(self.probs, self.v_big).astype(BF)
-        return self.z + self.rows(2) * nn(att, w_o[...])
+        left, right = w_o()
+        projected = jnp.concatenate([nn(att, left), nn(att, right)], axis=1)
+        return self.z + self.rows(2) * projected
 
     def backward(self, dout, w_q, w_k, w_v, w_o):
         t = self.tokens
-        datt = nt((self.rows(2) * dout).astype(BF), w_o[...]).astype(BF)
+        left, right = w_o()
+        cut = left.shape[1]
+        dproj = (self.rows(2) * dout).astype(BF)
+        datt = (nt(dproj[:, :cut], left) + nt(dproj[:, cut:], right)).astype(BF)
         dprobs = nt(datt, self.v_big)
         dv = self.fold(tn(self.probs, datt)).astype(BF)
         factor = self.head ** (-0.5)
@@ -139,7 +144,7 @@
         dq = norm_back(dqn, self.q, self.r_q).astype(BF)
         dk = norm_back(dkn, self.k, self.r_k).astype(BF)
         dlow = (nt(dq, self.up_q) + nt(dv, self.up_v)).astype(BF)
-        du = nt(dq, w_q[...]) + nt(dk, w_k[...]) + nt(dv, w_v[...]) + nn(dlow, self.down)
+        du = nt(dq, w_q()) + nt(dk, w_k()) + nt(dv, w_v()) + nn(dlow, self.down)
         du = du.astype(BF).astype(F32)
         grad_down = tn(dlow, self.u)
         grad_up = jnp.concatenate(
@@ -167,160 +172,214 @@
     return (row // span == col // span) & (row % positions == col % positions)
 
 
-def spatial_forward_kernel(positions, z, mod, down, up, w_in, w_out, hidden, q, k, v, low):
-    layer = Layer(z[...], mod, 0, down, up, 0, spatial_mask(z.shape[0], positions))
-    layer.project(w_in.at[0], w_in.at[1], w_in.at[2])
-    layer.attend()
-    hidden[...] = layer.output(w_out).astype(BF)
-    q[...], k[...], v[...], low[...] = layer.q, layer.k, layer.v, layer.low
-
-
-def temporal_kernel(positions, z, upstream, mod, down, up, w_in, w_out, dz, g_down, g_up):
-    layer = Layer(
-        z[...], mod, 3, down, up, 1, temporal_mask(z.shape[0], mod.shape[0], positions)
-    )
-    layer.project(w_in.at[0], w_in.at[1], w_in.at[2])
-    layer.attend()
-    grad, g_down[...], g_up[...] = layer.backward(
-        upstream[...].astype(F32), w_in.at[0], w_in.at[1], w_in.at[2], w_out
-    )
-    dz[...] = grad.astype(BF)
-
-
-def spatial_backward_kernel(
-    positions, z, cotangent, q, k, v, low, mod, down, up, w_in, w_out, dz, g_down, g_up
-):
-    layer = Layer(z[...], mod, 0, down, up, 0, spatial_mask(z.shape[0], positions))
-    layer.q, layer.k, layer.v, layer.low = q[...], k[...], v[...], low[...]
-    layer.attend()
-    grad, g_down[...], g_up[...] = layer.backward(
-        cotangent[...].astype(F32), w_in.at[0], w_in.at[1], w_in.at[2], w_out
-    )
-    dz[...] = grad.astype(BF)
-
-
-def vmem_call(kernel, out_shape, *operands):
-    return pl.pallas_call(
-        kernel,
-        out_shape=out_shape,
-        in_specs=[VMEM] * len(operands),
-        out_specs=[VMEM] * len(out_shape),
-        compiler_params=pltpu.CompilerParams(vmem_limit_bytes=VMEM_BYTES),
-    )(*operands)
-
-
-def gather_kernel(
-    n_dp, n_seq, in_s, out_s, in_t, out_t, all_in_s, all_out_s, all_in_t, all_out_t, own_sem,
-    sib_send, sib_recv, x_send, x_recv, y_send, y_recv, fwd_send, fwd_recv,
+def flip1(i):
+    return i + 1 - 2 * (i % 2)
+
+
+def flip2(i):
+    return i + 2 - 4 * ((i // 2) % 2)
+
+
+def layers_kernel(
+    n_dp, n_seq, positions, z, upstream, mod, down, up, stack_s, stack_t, grad, down_s, up_s,
+    down_t, up_t, w, sent_hidden, got_hidden, sent_back, got_back, own_sem, sib_send, sib_recv,
+    a_send, a_recv, y_send, y_recv, z_send, z_recv, c_send, c_recv, f_send, f_recv, h_send,
+    h_recv, b_send, b_recv,
 ):
     d, s = lax.axis_index("dp"), lax.axis_index("seq")
     chips = n_seq // 2
     chip, core = s // 2, s % 2
-    other_core = 2 * chip + 1 - core
-    pair = d + 1 - 2 * (d % 2)
-
-    def at(chip_index):
-        return 2 * lax.rem(chip_index + chips, chips)
+    sibling = (d, flip1(s))
+    by_y, by_z = (flip1(d), s), (flip2(d), s)
+    piece = d % 4
+    hops = range(1, chips)
+
+    def far(j):
+        return 2 * lax.rem(chip + j + chips, chips) + core
+
+    def seq_at(j):
+        return lax.rem(s + j, n_seq)
 
     barrier = pltpu.get_barrier_semaphore()
-    greet = [(d, other_core), (pair, s)] + [(d, at(chip + j) + core) for j in range(1, chips)]
+    greet = [by_y, by_z] + [(d, seq_at(j)) for j in range(1, n_seq)]
     for target in greet:
         pl.semaphore_signal(barrier, inc=1, device_id=target, device_id_type=MESH)
     pl.semaphore_wait(barrier, len(greet))
 
-    def source(piece):
-        mine, out = (in_s, out_s) if piece < 4 else (in_t, out_t)
-        return mine.at[piece % 4] if piece % 4 < 3 else out
-
-    def place(piece, shard):
-        full, out = (all_in_s, all_out_s) if piece < 4 else (all_in_t, all_out_t)
-        return full.at[piece % 4, shard] if piece % 4 < 3 else out.at[shard]
-
-    def remote(src, dst, send, recv, target):
+    def remote(source, dest, send, recv, target):
         return pltpu.make_async_remote_copy(
-            src_ref=src, dst_ref=dst, send_sem=send, recv_sem=recv,
-            device_id=target, device_id_type=MESH,
-        )
-
-    def own(piece):
-        return pltpu.make_async_copy(source(piece), place(piece, s), own_sem.at[piece])
-
-    def to_sibling(piece):
+            src_ref=source, dst_ref=dest, send_sem=send, recv_sem=recv, device_id=target,
+            device_id_type=MESH,
+        )
+
+    stacks = (stack_s, stack_t)
+
+    def own(l):
+        return pltpu.make_async_copy(stacks[l], w.at[l, :, s], own_sem.at[l])
+
+    def to_sibling(l):
+        return remote(stacks[l], w.at[l, :, s], sib_send.at[l], sib_recv.at[l], sibling)
+
+    def across(l, j):
         return remote(
-            source(piece), place(piece, s), sib_send.at[piece], sib_recv.at[piece], (d, other_core)
-        )
-
-    def across(j, piece):
-        return remote(
-            source(piece), place(piece, s), x_send.at[j - 1, piece], x_recv.at[j - 1, piece],
-            (d, at(chip + j) + core),
-        )
-
-    def relay(j, piece, sems, target):
-        held = place(piece, at(chip - j) + core)
-        return remote(held, held, sems[0].at[j - 1, piece], sems[1].at[j - 1, piece], target)
-
-    def to_pair(j, piece):
-        return relay(j, piece, (y_send, y_recv), (pair, s))
-
-    def to_core(j, piece):
-        return relay(j, piece, (fwd_send, fwd_recv), (d, other_core))
-
-    def run(half):
-        layers = [0, 4]
-        first = [[base + 2 * half, base + 2 * half + 1] for base in layers]
-        second = [[base + 2 - 2 * half, base + 3 - 2 * half] for base in layers]
-        for layer in range(2):
-            for piece in first[layer]:
-                for j in range(1, chips):
-                    across(j, piece).start()
-        for piece in range(8):
-            to_sibling(piece).start()
-            own(piece).start()
-        for layer in range(2):
-            for piece in first[layer]:
-                for j in range(1, chips):
-                    across(j, piece).wait_recv()
-                    to_pair(j, piece).start()
-                    to_core(j, piece).start()
-            for piece in second[layer]:
-                for j in range(1, chips):
-                    to_pair(j, piece).wait_recv()
-                    to_core(j, piece).start()
-        for piece in range(8):
-            to_sibling(piece).wait()
-            own(piece).wait()
-            for j in range(1, chips):
-                to_core(j, piece).wait()
-        for layer in range(2):
-            for piece in first[layer]:
-                for j in range(1, chips):
-                    across(j, piece).wait_send()
-                    to_pair(j, piece).wait_send()
-
-    for half in range(2):
-        pl.when(d % 2 == half)(functools.partial(run, half))
-
-
-def gather_weights(n_dp, n_seq, weights):
-    in_s, out_s, in_t, out_t = weights
-    links = max(n_seq // 2 - 1, 1)
-    dma = pltpu.SemaphoreType.DMA
-    shapes = []
-    for w in weights:
-        full = w.shape[:-2] + (n_seq,) + w.shape[-2:]
-        shapes.append(jax.ShapeDtypeStruct(full, BF))
-    gathered = pl.pallas_call(
-        functools.partial(gather_kernel, n_dp, n_seq),
-        out_shape=shapes,
-        in_specs=[ANY] * 4,
-        out_specs=[ANY] * 4,
-        scratch_shapes=[dma((8,))] * 3 + [dma((links, 8))] * 6,
-        compiler_params=pltpu.CompilerParams(collective_id=0, has_side_effects=True),
-    )(*weights)
-    return [
-        g.reshape(g.shape[:-3] + (g.shape[-3] * g.shape[-2], g.shape[-1])) for g in gathered
-    ]
+            stacks[l].at[piece], w.at[l, piece, s], a_send.at[l, j - 1], a_recv.at[l, j - 1],
+            (d, far(j)),
+        )
+
+    def pass_on(l, j, which, send, recv, target):
+        held = w.at[l, which, far(-j)]
+        return remote(held, held, send, recv, target)
+
+    def to_y(l, j):
+        return pass_on(l, j, piece, y_send.at[l, j - 1], y_recv.at[l, j - 1], by_y)
+
+    def to_z(l, j):
+        return pass_on(l, j, piece, z_send.at[l, j - 1], z_recv.at[l, j - 1], by_z)
+
+    corner_piece = jnp.where(core == 0, flip2(piece), flip1(piece))
+    corner_target = (jnp.where(core == 0, flip1(d), flip2(d)), s)
+
+    def to_corner(l, j):
+        return pass_on(
+            l, j, corner_piece, c_send.at[l, j - 1], c_recv.at[l, j - 1], corner_target
+        )
+
+    kinds = [piece, flip1(piece), flip2(piece), flip1(flip2(piece))]
+
+    def to_core(l, j, kind):
+        return pass_on(
+            l, j, kinds[kind], f_send.at[l, j - 1, kind], f_recv.at[l, j - 1, kind], sibling
+        )
+
+    def stage_first(l):
+        for j in hops:
+            across(l, j).start()
+
+    def stage_near(l):
+        to_sibling(l).start()
+        own(l).start()
+
+    def stage_pass(l):
+        for j in hops:
+            across(l, j).wait_recv()
+            to_y(l, j).start()
+            to_z(l, j).start()
+            to_core(l, j, 0).start()
+
+    def stage_corner(l):
+        for j in hops:
+            to_y(l, j).wait_recv()
+            to_z(l, j).wait_recv()
+            to_corner(l, j).start()
+            to_core(l, j, 1).start()
+            to_core(l, j, 2).start()
+
+    def stage_last(l):
+        for j in hops:
+            to_corner(l, j).wait_recv()
+            to_core(l, j, 3).start()
+        for j in hops:
+            for kind in range(4):
+                to_core(l, j, kind).wait_recv()
+        to_sibling(l).wait_recv()
+        own(l).wait()
+
+    inner = up.shape[3]
+    lanes = w.shape[4]
+    width = z.shape[1]
+    out_rows = w.shape[3] // 2
+
+    def loader(l, i):
+        return lambda: jnp.concatenate([w[l, i, k, :, :inner] for k in range(n_seq)], axis=0)
+
+    def out_loader(l):
+        def load():
+            left = [w[l, 3, k, :out_rows, :] for k in range(n_seq)]
+            right = [w[l, 3, k, out_rows:, : width - lanes] for k in range(n_seq)]
+            return jnp.concatenate(left, axis=0), jnp.concatenate(right, axis=0)
+
+        return load
+
+    def exchange(values, sent, got, send, recv):
+        batch, blocks, span = sent.shape[:3]
+        for b in range(batch):
+            for k in range(blocks):
+                start = (b * blocks + k) * span
+                sent[b, k] = values[start : start + span].astype(BF)
+        copies = [
+            remote(
+                sent.at[:, seq_at(j)], got.at[:, s], send.at[j - 1], recv.at[j - 1],
+                (d, seq_at(j)),
+            )
+            for j in range(1, n_seq)
+        ]
+        for copy in copies:
+            copy.start()
+        got[:, s] = sent[:, s]
+        return copies
+
+    def received(copies, got):
+        for copy in copies:
+            copy.wait_recv()
+        return jnp.concatenate(
+            [
+                got[b, k].astype(F32)
+                for b in range(got.shape[0])
+                for k in range(got.shape[1])
+            ],
+            axis=0,
+        )
+
+    stage_first(0)
+    stage_near(0)
+    tokens = z.shape[0]
+    first = Layer(z[...], mod, 0, down, up, 0, spatial_mask(tokens, positions))
+    stage_pass(0)
+    stage_first(1)
+    stage_near(1)
+    stage_corner(0)
+    stage_pass(1)
+    stage_last(0)
+    weights_s = [loader(0, i) for i in range(3)]
+    first.project(*weights_s)
+    first.attend()
+    hidden = first.output(out_loader(0))
+    out_copies = exchange(hidden, sent_hidden, got_hidden, h_send, h_recv)
+    stage_corner(1)
+    by_position = received(out_copies, got_hidden)
+    second = Layer(
+        by_position, mod, 3, down, up, 1,
+        temporal_mask(tokens, mod.shape[0], got_hidden.shape[2]),
+    )
+    stage_last(1)
+    weights_t = [loader(1, i) for i in range(3)]
+    second.project(*weights_t)
+    second.attend()
+    back, down_t[...], up_t[...] = second.backward(
+        upstream[...].astype(F32), *weights_t, out_loader(1)
+    )
+    back_copies = exchange(back, sent_back, got_back, b_send, b_recv)
+    by_frame = received(back_copies, got_back)
+    result, down_s[...], up_s[...] = first.backward(by_frame, *weights_s, out_loader(0))
+    grad[...] = result.astype(BF)
+    for copy in out_copies + back_copies:
+        copy.wait_send()
+    for l in range(2):
+        to_sibling(l).wait_send()
+        for j in hops:
+            across(l, j).wait_send()
+            to_y(l, j).wait_send()
+            to_z(l, j).wait_send()
+            to_corner(l, j).wait_send()
+            for kind in range(4):
+                to_core(l, j, kind).wait_send()
+
+
+def stacked(w_in, w_out, lanes):
+    left, right = w_out[:, :lanes], w_out[:, lanes:]
+    right = jnp.pad(right, ((0, 0), (0, lanes - right.shape[1])))
+    w_in = jnp.pad(w_in, ((0, 0), (0, 0), (0, lanes - w_in.shape[2])))
+    return jnp.concatenate([w_in, jnp.concatenate([left, right], axis=0)[None]], axis=0)
 
 
 def sum_kernel(
@@ -415,41 +474,36 @@
 
 
 def per_device(n_dp, n_seq, z, upstream, mod, in_s, out_s, in_t, out_t, down, up):
-    w_in_s, w_out_s, w_in_t, w_out_t = gather_weights(n_dp, n_seq, (in_s, out_s, in_t, out_t))
     batch, frames_here, positions, width = z.shape
     frames = frames_here * n_seq
-    positions_here = positions // n_seq
+    span = positions // n_seq
     inner, rank = up.shape[3], up.shape[2]
     tokens = batch * frames_here * positions
     factor = float(batch * n_dp * frames * positions) ** (-0.5)
+    lanes = -(-inner // 128) * 128
+    links = max(n_seq // 2 - 1, 1)
     shape = jax.ShapeDtypeStruct
-    z_rows = z.reshape(tokens, width)
-    hidden, q, k, v, low = vmem_call(
-        functools.partial(spatial_forward_kernel, positions),
-        [
-            shape((tokens, width), BF), shape((tokens, inner), F32), shape((tokens, inner), F32),
-            shape((tokens, inner), BF), shape((tokens, 2 * rank), BF),
-        ],
-        z_rows, mod, down, up, w_in_s, w_out_s,
-    )
-    by_position = lax.all_to_all(
-        hidden.reshape(z.shape), "seq", split_axis=2, concat_axis=1, tiled=True
-    )
-    grads = [
-        shape((tokens, width), BF), shape((2 * rank, width), F32), shape((2 * rank, inner), F32)
-    ]
-    back, down_t, up_t = vmem_call(
-        functools.partial(temporal_kernel, positions_here), grads,
-        by_position.reshape(tokens, width), upstream.reshape(tokens, width), mod, down, up,
-        w_in_t, w_out_t,
-    )
-    by_frame = lax.all_to_all(
-        back.reshape(batch, frames, positions_here, width), "seq", split_axis=1, concat_axis=2,
-        tiled=True,
-    )
-    grad, down_s, up_s = vmem_call(
-        functools.partial(spatial_backward_kernel, positions), grads,
-        z_rows, by_frame.reshape(tokens, width), q, k, v, low, mod, down, up, w_in_s, w_out_s,
+    dma = pltpu.SemaphoreType.DMA
+    buffer = pltpu.VMEM((batch, n_seq, span, width), BF)
+    pair, hop, lane = dma((2,)), dma((2, links)), dma((n_seq - 1,))
+    grads = [shape((2 * rank, width), F32), shape((2 * rank, inner), F32)]
+    grad, down_s, up_s, down_t, up_t = pl.pallas_call(
+        functools.partial(layers_kernel, n_dp, n_seq, positions),
+        out_shape=[shape((tokens, width), BF)] + grads * 2,
+        in_specs=[VMEM] * 5 + [ANY] * 2,
+        out_specs=[VMEM] * 5,
+        scratch_shapes=[pltpu.VMEM((2, 4, n_seq) + (in_s.shape[1], lanes), BF)]
+        + [buffer] * 4
+        + [pair] * 3
+        + [hop] * 8
+        + [dma((2, links, 4))] * 2
+        + [lane] * 4,
+        compiler_params=pltpu.CompilerParams(
+            collective_id=0, has_side_effects=True, vmem_limit_bytes=VMEM_BYTES
+        ),
+    )(
+        z.reshape(tokens, width), upstream.reshape(tokens, width), mod, down, up,
+        stacked(in_s, out_s, lanes), stacked(in_t, out_t, lanes),
     )
     flat = jnp.concatenate([a.reshape(-1) for a in (down_s, down_t, up_s, up_t)]) * factor
     flat = sum_everywhere(n_dp, n_seq, flat)

time: 185 us -> 110 us (0.59)
  Pallas kernels: 152 us -> 93.2 us
  blocking collectives: 9.34 us -> 0 us
  waiting for transfers between devices: 4.46 us -> 0 us
  starting transfers between devices: 3.99 us -> 0 us
  other arithmetic: 0.06 us -> 1.99 us
    pallas_call x4 -> x1, Pallas kernels: 122 us -> 64.9 us  [per_device(): pl.pallas_call(functools.partial(layers_kernel, n_dp, n_seq, positions),...]
    all_to_all x1 -> x0, blocking collectives: 9.34 us -> none  [per_device(): lax.all_to_all(hidden.reshape(z.shape), 'seq', split_axis=2, concat_axis=...]
    all_to_all x1 -> x0, waiting for transfers between devices: 4.46 us -> none  [per_device(): lax.all_to_all(back.reshape(batch, frames, positions_here, width), 'seq',...]
    all_to_all x1 -> x0, starting transfers between devices: 3.99 us -> none  [per_device(): lax.all_to_all(back.reshape(batch, frames, positions_here, width), 'seq',...]
    reshape x2 -> x0, local copies, waits for them, and re-layouts: 3.01 us -> none  [the longest x1 1.74 us: per_device(): back.reshape(batch, frames, positions_here, width)]
    slice x0 -> x6, local copies, waits for them, and re-layouts: none -> 1.87 us  [stacked(): left, right = (w_out[:, :lanes], w_out[:, lanes:])]
    concatenate x0 -> x1, other arithmetic: none -> 1.87 us  [stacked(): jnp.concatenate([w_in, jnp.concatenate([left, right], axis=0)[None]], axi...]
  transfers between devices with their start and end apart: 1 -> 0, of which waited for: 1 -> 0; matrix products, arithmetic and copies ran while one was open for 1% -> 0% of each run, Pallas kernels for 0% -> 0%
where the time goes in v2:
time: 110 us; the launch traced here: 109 us
  Pallas kernels  93.2 us (85%)
  local copies, waits for them, and re-layouts  13.1 us (12%)
  other arithmetic  1.99 us (2%)
    pallas_call x1, Pallas kernels, per_device(): pl.pallas_call(functools.partial(layers_kernel, n_dp, n_seq, positions),...  64.9 us
    pallas_call x1, Pallas kernels, sum_everywhere(): pl.pallas_call(functools.partial(sum_kernel, n_dp, n_seq), out_shape=jax....  28.3 us
    reshape x4, local copies, waits for them, and re-layouts, per_device(): a.reshape(-1)  4.01 us
    unnamed x8, local copies, waits for them, and re-layouts  2.33 us

profile of v2, /device:TPU:1, one launch (start us, length us, event | category | flops | bytes accessed | tf_op | source)
XLA Modules:
  0.0 109.1 jit_solution(12078790716821036706)
XLA Ops:
  0.6 0.0 slice-start
  0.6 0.0 slice-start.1
  0.7 0.0 copy-start.1
  0.7 0.0 copy-start
  0.7 1.6 %copy.12.mod = f32[2,6,1152]{2,1,0:T(8,128)} copy(f32[2,6,1152]{2,0,1:T(2,128)} %param.11) | data formatting | bytes 110592 | tf_op args[2]
  2.3 0.9 slice.22
  3.2 0.9 slice.21
  4.2 0.0 slice-done
  4.2 0.0 slice-done.1
  4.2 0.0 copy-done.1
  4.3 0.0 copy-done
  4.3 1.9 %fusion.2 = (bf16[4,288,640]{2,1,0:T(8,128)(2,1)}, bf16[4,288,640]{2,1,0:T(8,128)(2,1)}) fusion(bf16[3,288,576]{2,1,0:T(8,128)(2,1)S(1)} %copy-done, bf16[1,288,640]{2,1,0:T(8,128)(2,1)S(1)} %fusion.7, bf16[1,288,640]{2,1,0:T(8,128)(2,1)S(1)} %fusion.9, bf16[3,288,576]{2,1,0:T(8,128)(2,1)S(1)} %copy-done.1), kind=kLoop, calls=%fused_computation.3 | loop fusion | flops 8110080 | bytes 5677056 | tf_op jit(solution)/shard_map/concatenate | solution.py:382
  6.1 64.9 %shard_map.112 = (bf16[128,1152]{1,0:T(8,128)(2,1)}, f32[64,1152]{1,0:T(8,128)}, f32[64,576]{1,0:T(8,128)}, f32[64,1152]{1,0:T(8,128)}, f32[64,576]{1,0:T(8,128)}) custom-call(bf16[128,1152]{1,0:T(8,128)(2,1)} %bitcast.14, bf16[128,1152]{1,0:T(8,128)(2,1)} %bitcast.15, f32[2,6,1152]{2,1,0:T(8,128)} %copy.12.mod, f32[2,2,32,1152]{3,2,1,0:T(8,128)} %down.1, ...), custom_call_target="tpu_custom_call" | custom-call | tf_op jit(solution)/shard_map/pallas_call | solution.py:490
  71.0 1.0 reshape.44
  72.1 1.0 reshape.45
  73.1 1.0 reshape.42
  74.1 1.0 reshape.43
  75.1 0.1 maximum_multiply_fusion
  75.1 1.0 pad.22
  76.2 28.3 %shard_map.113 = f32[4,8,64,128]{3,2,1,0:T(8,128)} custom-call(f32[4,8,64,128]{3,2,1,0:T(8,128)} %bitcast.11), custom_call_target="tpu_custom_call" | custom-call | tf_op jit(solution)/shard_map/pallas_call | solution.py:456
  104.5 1.0 slice.28
  105.5 0.0 copy-start.2
  105.5 1.1 %slice.27 = f32[147456]{0:T(1024)S(1)} slice(f32[262144]{0:T(1024)} %bitcast.13), slice={[0:147456]} | slice | bytes 1179648 | tf_op jit(solution)/shard_map/slice | solution.py:511
  106.6 0.9 reshape.48
  107.6 0.8 reshape.49
  108.4 0.0 copy-done.2
  108.4 0.7 copy.15
  (2 shorter events, 0.1 us)
Async XLA Ops:
  0.6 3.6 %slice-start = ((bf16[144,1152]{1,0:T(8,128)(2,1)}), bf16[144,512]{1,0:T(8,128)(2,1)S(1)}, s32[]{:S(2)}) async-start(bf16[144,1152]{1,0:T(8,128)(2,1)} %param.15), calls=%async_computation | async-start | bytes 294912 | tf_op jit(solution)/shard_map/slice | solution.py:379
  0.6 3.6 %slice-start.1 = ((bf16[144,1152]{1,0:T(8,128)(2,1)}), bf16[144,640]{1,0:T(8,128)(2,1)S(1)}, s32[]{:S(2)}) async-start(bf16[144,1152]{1,0:T(8,128)(2,1)} %param.15), calls=%async_computation.1 | async-start | bytes 368640 | tf_op jit(solution)/shard_map/slice | solution.py:379
  0.7 3.6 %copy-start.1 = (bf16[3,288,576]{2,1,0:T(8,128)(2,1)S(1)}, bf16[3,288,576]{2,1,0:T(8,128)(2,1)}, u32[]{:S(2)}) copy-start(bf16[3,288,576]{2,1,0:T(8,128)(2,1)} %param.14) | copy-start | bytes 2985988
  0.7 3.6 %copy-start = (bf16[3,288,576]{2,1,0:T(8,128)(2,1)S(1)}, bf16[3,288,576]{2,1,0:T(8,128)(2,1)}, u32[]{:S(2)}) copy-start(bf16[3,288,576]{2,1,0:T(8,128)(2,1)} %param.12) | copy-start | bytes 2985988
  105.5 2.9 %copy-start.2 = (bf16[128,1152]{1,0:T(8,128)(2,1)S(1)}, bf16[128,1152]{1,0:T(8,128)(2,1)}, u32[]{:S(2)}) copy-start(bf16[128,1152]{1,0:T(8,128)(2,1)} %get-tuple-element.8) | copy-start | bytes 884740

commit v3 on v2

--- a/solution.py
+++ b/solution.py
@@ -181,10 +181,10 @@
 
 
 def layers_kernel(
-    n_dp, n_seq, positions, z, upstream, mod, down, up, stack_s, stack_t, grad, down_s, up_s,
-    down_t, up_t, w, sent_hidden, got_hidden, sent_back, got_back, own_sem, sib_send, sib_recv,
+    n_dp, n_seq, positions, factor, z, upstream, mod, down, up, stack_s, stack_t, grad,
+    all_down, all_up, w, wide, got_seq, part, got_dp, full, sent_hidden, got_hidden, sent_back, got_back, own_sem, sib_send, sib_recv,
     a_send, a_recv, y_send, y_recv, z_send, z_recv, c_send, c_recv, f_send, f_recv, h_send,
-    h_recv, b_send, b_recv,
+    h_recv, b_send, b_recv, s1, r1, s2, r2, s3, r3, s4, r4,
 ):
     d, s = lax.axis_index("dp"), lax.axis_index("seq")
     chips = n_seq // 2
@@ -200,8 +200,11 @@
     def seq_at(j):
         return lax.rem(s + j, n_seq)
 
+    def dp_at(j):
+        return lax.rem(d + j, n_dp)
+
     barrier = pltpu.get_barrier_semaphore()
-    greet = [by_y, by_z] + [(d, seq_at(j)) for j in range(1, n_seq)]
+    greet = [(dp_at(j), s) for j in range(1, n_dp)] + [(d, seq_at(j)) for j in range(1, n_seq)]
     for target in greet:
         pl.semaphore_signal(barrier, inc=1, device_id=target, device_id_type=MESH)
     pl.semaphore_wait(barrier, len(greet))
@@ -329,6 +332,96 @@
             ],
             axis=0,
         )
+
+    part_rows = wide.shape[3]
+    block_parts = down.shape[2] * 2 // part_rows
+    down_blocks = width // 128
+    up_blocks = -(-inner // 128)
+    used = (down_blocks + up_blocks) * block_parts
+    all_sends = []
+
+    def spot(p):
+        return p // n_dp, p % n_dp
+
+    def fan(count, source, dest, send, recv, target):
+        copies = [
+            remote(source(j), dest(j), send.at[j - 1], recv.at[j - 1], target(j))
+            for j in range(1, count)
+        ]
+        for copy in copies:
+            copy.start()
+        all_sends.extend(copies)
+        return copies
+
+    def to_seq(j):
+        return d, seq_at(j)
+
+    def to_dp(j):
+        return dp_at(j), s
+
+    def landed(copies):
+        for copy in copies:
+            copy.wait_recv()
+
+    def sum_first(l, grad_down, grad_up):
+        fill = jnp.zeros((grad_up.shape[0], up_blocks * 128 - inner), F32)
+        grad_up = jnp.concatenate([grad_up, fill], axis=1)
+        for p in range(n_dp * n_seq):
+            i, k = spot(p)
+            if p >= used:
+                wide[l, i, k] = jnp.zeros((part_rows, 128), BF)
+                continue
+            c, h = p // block_parts, p % block_parts
+            values = grad_down if c < down_blocks else grad_up
+            c = c if c < down_blocks else c - down_blocks
+            rows = values[h * part_rows : (h + 1) * part_rows, c * 128 : (c + 1) * 128]
+            wide[l, i, k] = rows.astype(BF)
+        return fan(
+            n_seq, lambda j: wide.at[l, seq_at(j)], lambda j: got_seq.at[l, j - 1],
+            s1.at[l], r1.at[l], to_seq,
+        )
+
+    def sum_second(l, copies):
+        landed(copies)
+        total = wide[l, s].astype(F32)
+        for j in range(1, n_seq):
+            total = total + got_seq[l, j - 1].astype(F32)
+        part[l] = total.astype(BF)
+        return fan(
+            n_dp, lambda j: part.at[l, dp_at(j)], lambda j: got_dp.at[l, j - 1],
+            s2.at[l], r2.at[l], to_dp,
+        )
+
+    def sum_third(l, copies):
+        landed(copies)
+        total = part[l, d].astype(F32)
+        for j in range(1, n_dp):
+            total = total + got_dp[l, j - 1].astype(F32)
+        full[l, s, d] = total.astype(BF)
+        return fan(
+            n_dp, lambda j: full.at[l, s, d], lambda j: full.at[l, s, d],
+            s3.at[l], r3.at[l], to_dp,
+        )
+
+    def sum_fourth(l, copies):
+        landed(copies)
+        return fan(
+            n_seq, lambda j: full.at[l, s], lambda j: full.at[l, s], s4.at[l], r4.at[l], to_seq
+        )
+
+    def sum_last(l, copies):
+        landed(copies)
+        for p in range(used):
+            i, k = spot(p)
+            c, h = p // block_parts, p % block_parts
+            rows = pl.ds(h * part_rows, part_rows)
+            values = full[l, i, k].astype(F32) * factor
+            if c < down_blocks:
+                all_down[l, rows, c * 128 : (c + 1) * 128] = values
+            else:
+                start = (c - down_blocks) * 128
+                stop = min(start + 128, inner)
+                all_up[l, rows, start:stop] = values[:, : stop - start]
 
     stage_first(0)
     stage_near(0)
@@ -355,14 +448,24 @@
     weights_t = [loader(1, i) for i in range(3)]
     second.project(*weights_t)
     second.attend()
-    back, down_t[...], up_t[...] = second.backward(
+    back, down_t, up_t = second.backward(
         upstream[...].astype(F32), *weights_t, out_loader(1)
     )
     back_copies = exchange(back, sent_back, got_back, b_send, b_recv)
+    sum_t = sum_first(1, down_t, up_t)
     by_frame = received(back_copies, got_back)
-    result, down_s[...], up_s[...] = first.backward(by_frame, *weights_s, out_loader(0))
+    sum_t = sum_second(1, sum_t)
+    result, down_s, up_s = first.backward(by_frame, *weights_s, out_loader(0))
+    sum_s = sum_first(0, down_s, up_s)
+    sum_t = sum_third(1, sum_t)
     grad[...] = result.astype(BF)
-    for copy in out_copies + back_copies:
+    sum_s = sum_second(0, sum_s)
+    sum_t = sum_fourth(1, sum_t)
+    sum_s = sum_third(0, sum_s)
+    sum_s = sum_fourth(0, sum_s)
+    sum_last(1, sum_t)
+    sum_last(0, sum_s)
+    for copy in out_copies + back_copies + all_sends:
         copy.wait_send()
     for l in range(2):
         to_sibling(l).wait_send()
@@ -380,97 +483,6 @@
     right = jnp.pad(right, ((0, 0), (0, lanes - right.shape[1])))
     w_in = jnp.pad(w_in, ((0, 0), (0, 0), (0, lanes - w_in.shape[2])))
     return jnp.concatenate([w_in, jnp.concatenate([left, right], axis=0)[None]], axis=0)
-
-
-def sum_kernel(
-    n_dp, n_seq, x, out, wide, got_seq, part, got_dp, full, s1, r1, s2, r2, s3, r3, s4, r4
-):
-    d, s = lax.axis_index("dp"), lax.axis_index("seq")
-
-    def seq_at(j):
-        return lax.rem(s + j, n_seq)
-
-    def dp_at(j):
-        return lax.rem(d + j, n_dp)
-
-    barrier = pltpu.get_barrier_semaphore()
-    for j in range(1, n_seq):
-        pl.semaphore_signal(barrier, inc=1, device_id=(d, seq_at(j)), device_id_type=MESH)
-    for j in range(1, n_dp):
-        pl.semaphore_signal(barrier, inc=1, device_id=(dp_at(j), s), device_id_type=MESH)
-    wide[...] = x[...].astype(BF)
-    pl.semaphore_wait(barrier, n_seq - 1 + n_dp - 1)
-
-    def exchange(count, source, dest, send, recv, target):
-        copies = [
-            pltpu.make_async_remote_copy(
-                src_ref=source(j), dst_ref=dest(j), send_sem=send.at[j - 1],
-                recv_sem=recv.at[j - 1], device_id=target(j), device_id_type=MESH,
-            )
-            for j in range(1, count)
-        ]
-        for copy in copies:
-            copy.start()
-        return copies
-
-    to_seq = lambda j: (d, seq_at(j))
-    to_dp = lambda j: (dp_at(j), s)
-    pending = exchange(
-        n_seq, lambda j: wide.at[seq_at(j)], lambda j: got_seq.at[j - 1], s1, r1, to_seq
-    )
-    for copy in pending:
-        copy.wait_recv()
-    total = x[s]
-    for j in range(1, n_seq):
-        total = total + got_seq[j - 1].astype(F32)
-    part[...] = total.astype(BF)
-    more = exchange(n_dp, lambda j: part.at[dp_at(j)], lambda j: got_dp.at[j - 1], s2, r2, to_dp)
-    for copy in more:
-        copy.wait_recv()
-    mine = part[d].astype(F32)
-    for j in range(1, n_dp):
-        mine = mine + got_dp[j - 1].astype(F32)
-    full[s, d] = mine.astype(BF)
-    pending += more
-    more = exchange(n_dp, lambda j: full.at[s, d], lambda j: full.at[s, d], s3, r3, to_dp)
-    for copy in more:
-        copy.wait_recv()
-    pending += more
-    more = exchange(n_seq, lambda j: full.at[s], lambda j: full.at[s], s4, r4, to_seq)
-    for copy in more:
-        copy.wait_recv()
-    out[...] = full[...].astype(F32)
-    for copy in pending + more:
-        copy.wait_send()
-
-
-def sum_everywhere(n_dp, n_seq, flat):
-    total = flat.shape[0]
-    unit = 16 * 128
-    devices = n_dp * n_seq
-    rows = -(-total // (devices * unit)) * 16
-    padded = jnp.pad(flat, (0, devices * rows * 128 - total))
-    shape = (n_seq, n_dp, rows, 128)
-    dma = pltpu.SemaphoreType.DMA
-    seq_sem, dp_sem = dma((n_seq - 1,)), dma((n_dp - 1,))
-    summed = pl.pallas_call(
-        functools.partial(sum_kernel, n_dp, n_seq),
-        out_shape=jax.ShapeDtypeStruct(shape, F32),
-        in_specs=[VMEM],
-        out_specs=VMEM,
-        scratch_shapes=[
-            pltpu.VMEM(shape, BF),
-            pltpu.VMEM((n_seq - 1,) + shape[1:], BF),
-            pltpu.VMEM(shape[1:], BF),
-            pltpu.VMEM((n_dp - 1,) + shape[2:], BF),
-            pltpu.VMEM(shape, BF),
-            seq_sem, seq_sem, dp_sem, dp_sem, dp_sem, dp_sem, seq_sem, seq_sem,
-        ],
-        compiler_params=pltpu.CompilerParams(
-            collective_id=1, has_side_effects=True, vmem_limit_bytes=VMEM_BYTES
-        ),
-    )(padded.reshape(shape))
-    return summed.reshape(-1)[:total]
 
 
 def per_device(n_dp, n_seq, z, upstream, mod, in_s, out_s, in_t, out_t, down, up):
@@ -486,18 +498,31 @@
     dma = pltpu.SemaphoreType.DMA
     buffer = pltpu.VMEM((batch, n_seq, span, width), BF)
     pair, hop, lane = dma((2,)), dma((2, links)), dma((n_seq - 1,))
-    grads = [shape((2 * rank, width), F32), shape((2 * rank, inner), F32)]
-    grad, down_s, up_s, down_t, up_t = pl.pallas_call(
-        functools.partial(layers_kernel, n_dp, n_seq, positions),
-        out_shape=[shape((tokens, width), BF)] + grads * 2,
+    grads = [shape((2, 2 * rank, width), F32), shape((2, 2 * rank, inner), F32)]
+    needed = 2 * rank * (width // 128 + -(-inner // 128))
+    part_rows = 16
+    while part_rows * n_dp * n_seq < needed:
+        part_rows *= 2
+    part = (part_rows, 128)
+    seq_sem, dp_sem = dma((2, n_seq - 1)), dma((2, n_dp - 1))
+    grad, all_down, all_up = pl.pallas_call(
+        functools.partial(layers_kernel, n_dp, n_seq, positions, factor),
+        out_shape=[shape((tokens, width), BF)] + grads,
         in_specs=[VMEM] * 5 + [ANY] * 2,
-        out_specs=[VMEM] * 5,
+        out_specs=[VMEM] * 3,
         scratch_shapes=[pltpu.VMEM((2, 4, n_seq) + (in_s.shape[1], lanes), BF)]
+        + [
+            pltpu.VMEM((2,) + lead + part, BF)
+            for lead in ((n_seq, n_dp), (n_seq - 1, n_dp), (n_dp,), (n_dp - 1,), (n_seq, n_dp))
+        ]
         + [buffer] * 4
         + [pair] * 3
         + [hop] * 8
         + [dma((2, links, 4))] * 2
-        + [lane] * 4,
+        + [lane] * 4
+        + [seq_sem] * 2
+        + [dp_sem] * 4
+        + [seq_sem] * 2,
         compiler_params=pltpu.CompilerParams(
             collective_id=0, has_side_effects=True, vmem_limit_bytes=VMEM_BYTES
         ),
@@ -505,10 +530,7 @@
         z.reshape(tokens, width), upstream.reshape(tokens, width), mod, down, up,
         stacked(in_s, out_s, lanes), stacked(in_t, out_t, lanes),
     )
-    flat = jnp.concatenate([a.reshape(-1) for a in (down_s, down_t, up_s, up_t)]) * factor
-    flat = sum_everywhere(n_dp, n_seq, flat)
-    cut = down.size
-    return grad.reshape(z.shape), flat[:cut].reshape(down.shape), flat[cut:].reshape(up.shape)
+    return grad.reshape(z.shape), all_down.reshape(down.shape), all_up.reshape(up.shape)
 
 
 def solution(mesh):

time: 110 us -> 96.4 us (0.88)
  Pallas kernels: 93.2 us -> 85.6 us
  local copies, waits for them, and re-layouts: 13.1 us -> 7.87 us
    pallas_call x2 -> x1, Pallas kernels: 93.2 us -> 85.6 us  [per_device(): pl.pallas_call(functools.partial(layers_kernel, n_dp, n_seq, positions, f...]
    reshape x6 -> x0, local copies, waits for them, and re-layouts: 5.78 us -> none  [the longest x4 4.01 us: per_device(): a.reshape(-1)]
    unnamed x8 -> x10, local copies, waits for them, and re-layouts: 2.33 us -> 6 us
    slice x2 -> x0, local copies, waits for them, and re-layouts: 2.13 us -> none  [the longest x1 1.15 us: per_device(): flat[:cut].reshape(down.shape)]
where the time goes in v3:
time: 96.4 us; the launch traced here: 96.1 us
  Pallas kernels  85.6 us (89%)
  local copies, waits for them, and re-layouts  7.87 us (8%)
  other arithmetic  1.93 us (2%)
    pallas_call x1, Pallas kernels, per_device(): pl.pallas_call(functools.partial(layers_kernel, n_dp, n_seq, positions, f...  85.6 us
    unnamed x10, local copies, waits for them, and re-layouts  6 us

profile of v3, /device:TPU:1, one launch (start us, length us, event | category | flops | bytes accessed | tf_op | source)
XLA Modules:
  0.0 96.1 jit_solution(6098363936196192684)
XLA Ops:
  0.6 0.0 slice-start
  0.6 0.0 slice-start.1
  0.7 0.0 copy-start.1
  0.7 0.0 copy-start
  0.7 1.6 %copy.12.mod = f32[2,6,1152]{2,1,0:T(8,128)} copy(f32[2,6,1152]{2,0,1:T(2,128)} %param.11) | data formatting | bytes 110592 | tf_op args[2]
  2.3 0.9 slice.13
  3.2 0.9 slice.12
  4.2 0.0 slice-done
  4.2 0.0 slice-done.1
  4.2 0.0 copy-done.1
  4.3 0.0 copy-done
  4.3 1.9 %fusion.2 = (bf16[4,288,640]{2,1,0:T(8,128)(2,1)}, bf16[4,288,640]{2,1,0:T(8,128)(2,1)}) fusion(bf16[3,288,576]{2,1,0:T(8,128)(2,1)S(1)} %copy-done, bf16[1,288,640]{2,1,0:T(8,128)(2,1)S(1)} %fusion.7, bf16[1,288,640]{2,1,0:T(8,128)(2,1)S(1)} %fusion.9, bf16[3,288,576]{2,1,0:T(8,128)(2,1)S(1)} %copy-done.1), kind=kLoop, calls=%fused_computation.3 | loop fusion | flops 8110080 | bytes 5677056 | tf_op jit(solution)/shard_map/concatenate | solution.py:485
  6.1 85.6 %shard_map.112 = (bf16[128,1152]{1,0:T(8,128)(2,1)}, f32[2,64,1152]{2,1,0:T(8,128)}, f32[2,64,576]{2,1,0:T(8,128)}) custom-call(bf16[128,1152]{1,0:T(8,128)(2,1)} %bitcast.13, bf16[128,1152]{1,0:T(8,128)(2,1)} %bitcast.14, f32[2,6,1152]{2,1,0:T(8,128)} %copy.12.mod, f32[2,2,32,1152]{3,2,1,0:T(8,128)} %down.1, f32[2,2,32,576]{3,2,1,0:T(8,128)} %up.1, ...), custom_call_target="tpu_custom_call" | custom-call | tf_op jit(solution)/shard_map/pallas_call | solution.py:508
  91.7 0.0 copy-start.2
  91.7 1.7 %copy.17 = bf16[2,1,64,1152]{3,2,1,0:T(8,128)(2,1)} copy(bf16[2,1,64,1152]{3,2,1,0:T(8,128)(2,1)} %bitcast.15) | data formatting | bytes 589824
  93.5 1.9 %copy.18 = f32[2,2,32,1152]{3,2,1,0:T(8,128)} copy(f32[2,2,32,1152]{3,2,1,0:T(8,128)} %bitcast.11) | data formatting | bytes 1179648
  95.4 0.0 copy-done.2
  95.4 0.7 copy.19
  (2 shorter events, 0.1 us)
Async XLA Ops:
  0.6 3.6 %slice-start = ((bf16[144,1152]{1,0:T(8,128)(2,1)}), bf16[144,512]{1,0:T(8,128)(2,1)S(1)}, s32[]{:S(2)}) async-start(bf16[144,1152]{1,0:T(8,128)(2,1)} %param.15), calls=%async_computation | async-start | bytes 294912 | tf_op jit(solution)/shard_map/slice | solution.py:482
  0.6 3.6 %slice-start.1 = ((bf16[144,1152]{1,0:T(8,128)(2,1)}), bf16[144,640]{1,0:T(8,128)(2,1)S(1)}, s32[]{:S(2)}) async-start(bf16[144,1152]{1,0:T(8,128)(2,1)} %param.15), calls=%async_computation.1 | async-start | bytes 368640 | tf_op jit(solution)/shard_map/slice | solution.py:482
  0.7 3.6 %copy-start.1 = (bf16[3,288,576]{2,1,0:T(8,128)(2,1)S(1)}, bf16[3,288,576]{2,1,0:T(8,128)(2,1)}, u32[]{:S(2)}) copy-start(bf16[3,288,576]{2,1,0:T(8,128)(2,1)} %param.14) | copy-start | bytes 2985988
  0.7 3.6 %copy-start = (bf16[3,288,576]{2,1,0:T(8,128)(2,1)S(1)}, bf16[3,288,576]{2,1,0:T(8,128)(2,1)}, u32[]{:S(2)}) copy-start(bf16[3,288,576]{2,1,0:T(8,128)(2,1)} %param.12) | copy-start | bytes 2985988
  91.7 3.7 %copy-start.2 = (f32[2,64,576]{2,1,0:T(8,128)S(1)}, f32[2,64,576]{2,1,0:T(8,128)}, u32[]{:S(2)}) copy-start(f32[2,64,576]{2,1,0:T(8,128)} %get-tuple-element.8) | copy-start | bytes 884740

commit v4 on v3

--- a/solution.py
+++ b/solution.py
@@ -192,7 +192,12 @@
     sibling = (d, flip1(s))
     by_y, by_z = (flip1(d), s), (flip2(d), s)
     piece = d % 4
-    hops = range(1, chips)
+    cuts = 2 if w.shape[3] % 32 == 0 else 1
+    rows_each = w.shape[3] // cuts
+    hops = range(cuts, chips * cuts)
+
+    def span_of(j):
+        return pl.ds(j % cuts * rows_each, rows_each)
 
     def far(j):
         return 2 * lax.rem(chip + j + chips, chips) + core
@@ -225,33 +230,33 @@
 
     def across(l, j):
         return remote(
-            stacks[l].at[piece], w.at[l, piece, s], a_send.at[l, j - 1], a_recv.at[l, j - 1],
-            (d, far(j)),
+            stacks[l].at[piece, span_of(j)], w.at[l, piece, s, span_of(j)],
+            a_send.at[l, j - cuts], a_recv.at[l, j - cuts], (d, far(j // cuts)),
         )
 
     def pass_on(l, j, which, send, recv, target):
-        held = w.at[l, which, far(-j)]
+        held = w.at[l, which, far(-(j // cuts)), span_of(j)]
         return remote(held, held, send, recv, target)
 
     def to_y(l, j):
-        return pass_on(l, j, piece, y_send.at[l, j - 1], y_recv.at[l, j - 1], by_y)
+        return pass_on(l, j, piece, y_send.at[l, j - cuts], y_recv.at[l, j - cuts], by_y)
 
     def to_z(l, j):
-        return pass_on(l, j, piece, z_send.at[l, j - 1], z_recv.at[l, j - 1], by_z)
+        return pass_on(l, j, piece, z_send.at[l, j - cuts], z_recv.at[l, j - cuts], by_z)
 
     corner_piece = jnp.where(core == 0, flip2(piece), flip1(piece))
     corner_target = (jnp.where(core == 0, flip1(d), flip2(d)), s)
 
     def to_corner(l, j):
         return pass_on(
-            l, j, corner_piece, c_send.at[l, j - 1], c_recv.at[l, j - 1], corner_target
+            l, j, corner_piece, c_send.at[l, j - cuts], c_recv.at[l, j - cuts], corner_target
         )
 
     kinds = [piece, flip1(piece), flip2(piece), flip1(flip2(piece))]
 
     def to_core(l, j, kind):
         return pass_on(
-            l, j, kinds[kind], f_send.at[l, j - 1, kind], f_recv.at[l, j - 1, kind], sibling
+            l, j, kinds[kind], f_send.at[l, j - cuts, kind], f_recv.at[l, j - cuts, kind], sibling
         )
 
     def stage_first(l):
@@ -493,7 +498,7 @@
     tokens = batch * frames_here * positions
     factor = float(batch * n_dp * frames * positions) ** (-0.5)
     lanes = -(-inner // 128) * 128
-    links = max(n_seq // 2 - 1, 1)
+    links = 2 * max(n_seq // 2 - 1, 1)
     shape = jax.ShapeDtypeStruct
     dma = pltpu.SemaphoreType.DMA
     buffer = pltpu.VMEM((batch, n_seq, span, width), BF)

time: 96.4 us -> 91.8 us (0.952)
  Pallas kernels: 85.6 us -> 81 us
    pallas_call x1, Pallas kernels: 85.6 us -> 81 us  [per_device(): pl.pallas_call(functools.partial(layers_kernel, n_dp, n_seq, positions, f...]
where the time goes in v4:
time: 91.8 us; the launch traced here: 91.5 us
  Pallas kernels  81 us (88%)
  local copies, waits for them, and re-layouts  7.87 us (9%)
  other arithmetic  1.93 us (2%)
    pallas_call x1, Pallas kernels, per_device(): pl.pallas_call(functools.partial(layers_kernel, n_dp, n_seq, positions, f...  81 us
    unnamed x10, local copies, waits for them, and re-layouts  6 us
    slice x6, local copies, waits for them, and re-layouts, stacked(): left, right = (w_out[:, :lanes], w_out[:, lanes:])  1.87 us
    concatenate x1, other arithmetic, stacked(): jnp.concatenate([w_in, jnp.concatenate([left, right], axis=0)[None]], axi...  1.87 us

profile of v4, /device:TPU:1, one launch (start us, length us, event | category | flops | bytes accessed | tf_op | source)
XLA Modules:
  0.0 91.5 jit_solution(18362221727007616893)
XLA Ops:
  0.6 0.0 slice-start
  0.6 0.0 slice-start.1
  0.7 0.0 copy-start.1
  0.7 0.0 copy-start
  0.7 1.6 %copy.12.mod = f32[2,6,1152]{2,1,0:T(8,128)} copy(f32[2,6,1152]{2,0,1:T(2,128)} %param.11) | data formatting | bytes 110592 | tf_op args[2]
  2.3 0.9 %slice.13 = bf16[144,512]{1,0:T(8,128)(2,1)S(1)} slice(bf16[144,1152]{1,0:T(8,128)(2,1)} %param.13), slice={[0:144], [640:1152]} | slice | bytes 294912 | tf_op jit(solution)/shard_map/slice | solution.py:487
  3.2 0.9 %slice.12 = bf16[144,640]{1,0:T(8,128)(2,1)S(1)} slice(bf16[144,1152]{1,0:T(8,128)(2,1)} %param.13), slice={[0:144], [0:640]} | slice | bytes 368640 | tf_op jit(solution)/shard_map/slice | solution.py:487
  4.2 0.0 slice-done
  4.2 0.0 slice-done.1
  4.2 0.0 copy-done.1
  4.3 0.0 copy-done
  4.3 1.9 %fusion.2 = (bf16[4,288,640]{2,1,0:T(8,128)(2,1)}, bf16[4,288,640]{2,1,0:T(8,128)(2,1)}) fusion(bf16[3,288,576]{2,1,0:T(8,128)(2,1)S(1)} %copy-done, bf16[1,288,640]{2,1,0:T(8,128)(2,1)S(1)} %fusion.7, bf16[1,288,640]{2,1,0:T(8,128)(2,1)S(1)} %fusion.9, bf16[3,288,576]{2,1,0:T(8,128)(2,1)S(1)} %copy-done.1), kind=kLoop, calls=%fused_computation.3 | loop fusion | flops 8110080 | bytes 5677056 | tf_op jit(solution)/shard_map/concatenate | solution.py:490
  6.1 81.0 %shard_map.112 = (bf16[128,1152]{1,0:T(8,128)(2,1)}, f32[2,64,1152]{2,1,0:T(8,128)}, f32[2,64,576]{2,1,0:T(8,128)}) custom-call(bf16[128,1152]{1,0:T(8,128)(2,1)} %bitcast.13, bf16[128,1152]{1,0:T(8,128)(2,1)} %bitcast.14, f32[2,6,1152]{2,1,0:T(8,128)} %copy.12.mod, f32[2,2,32,1152]{3,2,1,0:T(8,128)} %down.1, f32[2,2,32,576]{3,2,1,0:T(8,128)} %up.1, ...), custom_call_target="tpu_custom_call" | custom-call | tf_op jit(solution)/shard_map/pallas_call | solution.py:513
  87.1 0.0 copy-start.2
  87.1 1.7 %copy.17 = bf16[2,1,64,1152]{3,2,1,0:T(8,128)(2,1)} copy(bf16[2,1,64,1152]{3,2,1,0:T(8,128)(2,1)} %bitcast.15) | data formatting | bytes 589824
  88.8 1.9 %copy.18 = f32[2,2,32,1152]{3,2,1,0:T(8,128)} copy(f32[2,2,32,1152]{3,2,1,0:T(8,128)} %bitcast.11) | data formatting | bytes 1179648
  90.8 0.0 copy-done.2
  90.8 0.7 copy.19
  (2 shorter events, 0.1 us)
Async XLA Ops:
  0.6 3.6 %slice-start = ((bf16[144,1152]{1,0:T(8,128)(2,1)}), bf16[144,512]{1,0:T(8,128)(2,1)S(1)}, s32[]{:S(2)}) async-start(bf16[144,1152]{1,0:T(8,128)(2,1)} %param.15), calls=%async_computation | async-start | bytes 294912 | tf_op jit(solution)/shard_map/slice | solution.py:487
  0.6 3.6 %slice-start.1 = ((bf16[144,1152]{1,0:T(8,128)(2,1)}), bf16[144,640]{1,0:T(8,128)(2,1)S(1)}, s32[]{:S(2)}) async-start(bf16[144,1152]{1,0:T(8,128)(2,1)} %param.15), calls=%async_computation.1 | async-start | bytes 368640 | tf_op jit(solution)/shard_map/slice | solution.py:487
  0.7 3.6 %copy-start.1 = (bf16[3,288,576]{2,1,0:T(8,128)(2,1)S(1)}, bf16[3,288,576]{2,1,0:T(8,128)(2,1)}, u32[]{:S(2)}) copy-start(bf16[3,288,576]{2,1,0:T(8,128)(2,1)} %param.14) | copy-start | bytes 2985988
  0.7 3.6 %copy-start = (bf16[3,288,576]{2,1,0:T(8,128)(2,1)S(1)}, bf16[3,288,576]{2,1,0:T(8,128)(2,1)}, u32[]{:S(2)}) copy-start(bf16[3,288,576]{2,1,0:T(8,128)(2,1)} %param.12) | copy-start | bytes 2985988
  87.1 3.7 %copy-start.2 = (f32[2,64,576]{2,1,0:T(8,128)S(1)}, f32[2,64,576]{2,1,0:T(8,128)}, u32[]{:S(2)}) copy-start(f32[2,64,576]{2,1,0:T(8,128)} %get-tuple-element.8) | copy-start | bytes 884740
